TPU v7x, 32 devices: a whole 2x2x4 slice. The times are simulated.
32 devices in a mesh: groups: 2 (over x), op: 16 (over z, y, core).
Axes of the slice: x: 2, y: 2, z: 4, core: 2. Of those that a mesh axis runs over, the one named last changes fastest.
Arguments:
- psi: bfloat16 [32, 256, 256], P(('groups', 'op')), parts along dimension 0, may hold values from -60 to 60
- left_ops: bfloat16 [256, 256, 256], P(('groups', 'op')), parts along dimension 0, may hold values from -0.375 to 0.375
- right_ops: bfloat16 [256, 256, 256], P(('groups', 'op')), parts along dimension 0, may hold values from -0.03125 to 0.03125
- pair_term: int32 [2048], P('op'), may hold values from 0 to 127, as said below
- pair_source: int32 [2048], P('op'), may hold values from 0 to 15, as said below
- pair_target: int32 [2048], P('op'), may hold values from 0 to 15, as said below
- right_order: int32 [16], replicated, may hold values from 0 to 15, as said below
Outputs:
- sigma_one: bfloat16 [32, 256, 256], P(('groups', 'op')), parts along dimension 0
- sigma_two: bfloat16 [32, 256, 256], P(('groups', 'op')), parts along dimension 0
There are 2 independent parts, one for each index of `groups`. A program takes and returns all parts, laid end to end along the dimension named above; an argument that names none is the same for every part. Nothing has to cross between parts.
Inputs may be any that keep to these rules, and one draw needn't show every extreme that they name: `pair_term`: pair p names a term of the same device's block: from (p // 128) * 8 to that plus 8 - 1. `pair_source`: every sector is read by exactly 128 pairs. `pair_target`: every sector receives exactly 128 pairs; with M = 16, the pairs of block d (pairs d * 128 to d * 128 + 127) add only to sectors whose position j in right_order satisfies j // 1 in d, d + 1, d - 1, d + M // 2, counted modulo M, and 32 of them to each of these four. `right_order`: each sector number appears once.
All inputs are finite; a program needn't handle non-finite values.
Results may differ from a plain program's by a relative error of at most 0.0062.
Values may be sent and summed in bfloat16 or wider, within the bound.
No kernel may reach another device: no remote copies, remote signals or barrier semaphores. Data moves between devices by JAX's collectives and lax.ppermute only.
A program may use at most 192 MiB of HBM per device.

v0:
```python
import functools

import jax
import jax.numpy as jnp
from jax import lax
from jax.experimental import pallas as pl
from jax.experimental.pallas import tpu as pltpu
from jax.sharding import PartitionSpec as P

STRIP = 16
VMEM = pltpu.VMEM
SMEM = pltpu.SMEM
BF16 = jnp.bfloat16
F32 = jnp.float32
STEP = 1 << 32


def in_vmem(x):
    return pltpu.with_memory_space_constraint(x, VMEM)


def in_hbm(x):
    return pltpu.with_memory_space_constraint(x, pltpu.HBM)


def spec(n):
    return [pl.BlockSpec(memory_space=VMEM)] * n


def params(mib):
    return pltpu.CompilerParams(vmem_limit_bytes=mib << 20)


def cost(flops):
    return pl.CostEstimate(flops=flops, bytes_accessed=1, transcendentals=0)


def fold_sum(x):
    return jnp.sum(x.reshape(x.shape[0] // 8, 8, x.shape[1]), axis=0)


def prepare_body(count, me_ref, order, term, source, target, psi, left, right, *refs):
    outs, (psi_out, left_out, right_out) = refs[:8], refs[8:11]
    order_ref, term_ref, source_ref, target_ref, sems = refs[11:]
    copies = [
        pltpu.make_async_copy(a, b, sems.at[i])
        for i, (a, b) in enumerate(
            (
                (order, order_ref),
                (term, term_ref),
                (source, source_ref),
                (target, target_ref),
                (psi, psi_out),
                (left, left_out),
                (right, right_out),
            )
        )
    ]
    for copy in copies:
        copy.start()
    for copy in copies[:4]:
        copy.wait()
    me = me_ref[0]
    terms = left.shape[0]
    place = jnp.zeros(target_ref.shape, jnp.int32)
    source_place = jnp.zeros(source_ref.shape, jnp.int32)
    for j in range(count):
        place = jnp.where(target_ref[...] == order_ref[j], j, place)
        source_place = jnp.where(source_ref[...] == order_ref[j], j, source_place)
    local_term = term_ref[...] - me * terms
    pairs = term_ref.shape[1]
    width = count * STRIP
    columns = lax.broadcasted_iota(jnp.int32, (width, pairs), 0) // STRIP
    rows = lax.broadcasted_iota(jnp.int32, (terms * STRIP, pairs), 0) // STRIP
    owners = (jnp.bitwise_xor(me, count // 2), other_of(me, count), jnp.bitwise_xor(me, 1), me)
    same = (
        lax.broadcasted_iota(jnp.int32, (terms * STRIP, width), 0) % STRIP
        == lax.broadcasted_iota(jnp.int32, (terms * STRIP, width), 1) % STRIP
    )
    for application, sectors in enumerate((source_ref[...], source_place)):
        read = (columns == jnp.bitwise_xor(sectors, me)).astype(F32).astype(BF16)
        for slot, owner in enumerate(owners):
            hit = (rows == local_term) & (place == owner)
            counts = lax.dot_general(
                hit.astype(F32).astype(BF16), read, (((1,), (1,)), ((), ())), preferred_element_type=F32
            )
            outs[application * 4 + slot][...] = jnp.where(same, counts, 0.0).astype(BF16)
    for copy in copies[4:]:
        copy.wait()


def prepare(count, me, order, term, source, target, psi, left_ops, right_ops):
    pairs, terms = term.shape[0], left_ops.shape[0]
    results = pl.pallas_call(
        functools.partial(prepare_body, count),
        out_shape=[pltpu.VMEM((terms * STRIP, count * STRIP), BF16)] * 8
        + [pltpu.VMEM(x.shape, BF16) for x in (psi, left_ops, right_ops)],
        in_specs=[pl.BlockSpec(memory_space=SMEM)] + [pl.BlockSpec(memory_space=pl.ANY)] * 7,
        out_specs=spec(11),
        scratch_shapes=[pltpu.SMEM((count,), jnp.int32)]
        + [pltpu.VMEM((1, pairs), jnp.int32)] * 3
        + [pltpu.SemaphoreType.DMA((7,))],
        cost_estimate=cost(1),
        compiler_params=params(8),
    )(
        me.reshape(1),
        *[in_hbm(x) for x in (order, *[x.reshape(1, pairs) for x in (term, source, target)], psi, left_ops, right_ops)],
    )
    return results[:4], results[4:8], results[8], results[9], results[10]


def products(w_refs, left_ref, right_ref, blocks, outs, mixed, inner):
    terms, size = right_ref.shape[0], right_ref.shape[1]
    slots = len(w_refs)
    weights = jnp.concatenate([w[...] for w in w_refs], axis=0)
    for strip in range(size // STRIP):
        rows = slice(strip * STRIP, (strip + 1) * STRIP)
        stacked = jnp.concatenate([block[rows, :] for block in blocks], axis=0)
        value = jnp.dot(weights, stacked, preferred_element_type=F32)
        mixed[:, :, rows, :] = value.astype(BF16).reshape(slots, terms, STRIP, size)
    for k in range(terms):
        stacked = jnp.concatenate([mixed[t, k] for t in range(slots)], axis=0)
        value = jnp.dot(stacked, right_ref[k], preferred_element_type=F32).astype(BF16)
        for t in range(slots):
            inner[t, k * size : (k + 1) * size, :] = value[t * size : (t + 1) * size]
    for t in range(slots):
        row = jnp.concatenate([left_ref[k] for k in range(terms)], axis=1)
        total = jnp.dot(row, inner[t], preferred_element_type=F32)
        outs[t][...] = total.astype(outs[t].dtype)


def sums_body(count, slots, *refs):
    w_refs, (left_ref, right_ref), refs = refs[:slots], refs[slots : slots + 2], refs[slots + 2 :]
    products(w_refs, left_ref, right_ref, refs[:count], refs[count:-2], *refs[-2:])


def sums(weights, left_ops, right_ops, blocks, types):
    count, slots, (terms, size, _) = len(blocks), len(types), right_ops.shape
    return pl.pallas_call(
        functools.partial(sums_body, count, slots),
        out_shape=[pltpu.VMEM((size, size), t) for t in types],
        in_specs=spec(2 + slots + count),
        out_specs=spec(slots),
        scratch_shapes=[
            pltpu.VMEM((slots, terms, size, size), BF16),
            pltpu.VMEM((slots, terms * size, size), BF16),
        ],
        cost_estimate=cost(1),
        compiler_params=params(12),
    )(*[in_vmem(x) for x in (*weights, left_ops, right_ops, *blocks)])


def small(body, shapes, inputs, flops=1):
    return pl.pallas_call(
        body,
        out_shape=shapes,
        in_specs=spec(len(inputs)),
        out_specs=spec(len(shapes)),
        cost_estimate=cost(flops),
        compiler_params=params(8),
    )(*[in_vmem(x) for x in inputs])


def keep_body(count, *refs):
    blocks, stack, squares = refs[:count], refs[count], refs[count + 1]
    total = jnp.zeros((8, stack.shape[2]), F32)
    for m in range(count):
        value = blocks[m][...]
        stack[m] = value
        wide = value.astype(F32)
        total = total + fold_sum(wide * wide)
    squares[...] = jnp.broadcast_to(jnp.sum(total, keepdims=True), squares.shape)


def overlap_body(count, me_ref, order_ref, stack, *refs):
    blocks, overlap = refs[:count], refs[count]
    me = me_ref[0]
    total = jnp.zeros((8, stack.shape[2]), F32)
    for m in range(count):
        sector = order_ref[jnp.bitwise_xor(me, m)]
        wave = stack[jnp.bitwise_xor(sector, me)].astype(F32)
        total = total + fold_sum(wave * blocks[m][...].astype(F32))
    overlap[...] = jnp.broadcast_to(jnp.sum(total, keepdims=True), overlap.shape)


def overlap_with(me, order, stack, blocks):
    count = len(blocks)
    return pl.pallas_call(
        functools.partial(overlap_body, count),
        out_shape=pltpu.VMEM((8, 128), F32),
        in_specs=[pl.BlockSpec(memory_space=SMEM)] * 2 + spec(1 + count),
        out_specs=spec(1)[0],
        cost_estimate=cost(1),
        compiler_params=params(8),
    )(me.reshape(1), order, in_vmem(stack), *[in_vmem(x) for x in blocks])


def add_body(total, part, out):
    out[...] = total[...] + part[...].astype(F32)


def add(total, part):
    return small(add_body, [pltpu.VMEM(total.shape, F32)], (total, part), STEP)[0]


def raw_body(total, part, raw, sent):
    value = total[...] + part[...].astype(F32)
    raw[...] = value
    sent[...] = value.astype(BF16)


def first_body(count, raw, squares, out):
    rms = jnp.sqrt(squares[:1, :1] / (count * raw.shape[0] * raw.shape[1]))
    out[0] = (raw[...] / rms).astype(BF16)


def second_body(count, total, part, raw, overlap, squares, out):
    rms = jnp.sqrt(squares[:1, :1] / (count * raw.shape[0] * raw.shape[1]))
    theta = overlap[:1, :1] / squares[:1, :1]
    value = total[...] + part[...].astype(F32)
    out[0] = ((value - theta * raw[...]) / rms).astype(BF16)


def other_of(device, count):
    step = jnp.where(device % 2 == 0, count - 1, 1)
    return lax.rem(device + step, count)


def swap(x, count, mask):
    return lax.ppermute(x, "op", [(i, i ^ mask) for i in range(count)])


def swap_other(x, count):
    return lax.ppermute(x, "op", [(i, (i + (1 if i % 2 else count - 1)) % count) for i in range(count)])


def gather_blocks(field, count, prepared=()):
    blocks = {0: field}
    half = count // 2
    for mask in range(2, half, 2):
        blocks[mask] = swap(field, count, mask)
    blocks[half] = swap(field, count, half)
    far = after(blocks[half], *prepared) if prepared else blocks[half]
    for mask in range(2, half, 2):
        blocks[half + mask] = swap(far, count, mask)
    for mask in range(0, count, 2):
        blocks[mask + 1] = swap(blocks[mask], count, 1)
    return [blocks[m] for m in range(count)]


def after(x, *earlier):
    return lax.optimization_barrier((x, *earlier))[0]


def on_device(count, psi, left_ops, right_ops, pair_term, pair_source, pair_target, right_order):
    field = psi[0]
    size = field.shape[0]
    me = lax.axis_index("op").astype(jnp.int32)
    first_w, second_w, psi_block, left, right = prepare(
        count, me, right_order, pair_term, pair_source, pair_target, field, left_ops, right_ops
    )

    def partial_sums(w, blocks):
        (far,) = sums(w[:1], left, right, blocks, (BF16,))
        (other,) = sums((after(w[1], far),), left, right, blocks, (BF16,))
        near, own = sums((after(w[2], other), w[3]), left, right, blocks, (BF16, F32))
        return own, near, (swap(far, count, count // 2), swap_other(other, count), swap(near, count, 1))

    blocks = gather_blocks(field, count, first_w)
    blocks[0] = psi_block
    own, near, (far_in, other_in, near_in) = partial_sums(first_w, blocks)
    blocks[0] = after(blocks[0], near)
    stack, squares = small(
        functools.partial(keep_body, count),
        [pltpu.VMEM((count, size, size), BF16), pltpu.VMEM((8, 128), F32)],
        blocks,
    )
    total = add(add(after(own, squares), far_in), other_in)
    raw, raw_sent = small(
        raw_body, [pltpu.VMEM(own.shape, F32), pltpu.VMEM(own.shape, BF16)], (total, near_in), STEP
    )

    blocks = gather_blocks(raw_sent, count)
    own, near, (far_in, other_in, near_in) = partial_sums(second_w, blocks)
    out_shape = [jax.ShapeDtypeStruct((1, size, size), BF16)]
    (first,) = small(functools.partial(first_body, count), out_shape, (after(raw, near), squares))
    blocks[0] = after(blocks[0], near)
    overlap = overlap_with(me, right_order, stack, blocks)
    own, first = lax.optimization_barrier((own, first))
    total = add(add(after(own, overlap), far_in), other_in)
    (second,) = small(
        functools.partial(second_body, count), out_shape, (total, near_in, raw, overlap, squares), STEP
    )
    return first, second


def solution(mesh):
    return jax.shard_map(
        functools.partial(on_device, mesh.shape["op"]),
        mesh=mesh,
        in_specs=(
            P(("groups", "op"), None, None),
            P(("groups", "op"), None, None),
            P(("groups", "op"), None, None),
            P("op"),
            P("op"),
            P("op"),
            P(),
        ),
        out_specs=(P(("groups", "op"), None, None), P(("groups", "op"), None, None)),
        check_vma=False,
    )
```

profile of v0, /device:TPU:0, one launch (start us, length us, event | category | flops | bytes accessed | tf_op | source)
XLA Modules:
  0.0 68.1 jit_solution(6707982059675247499)
XLA Ops:
  0.6 4.1 %collective-permute-start.7 = (bf16[256,256]{1,0:T(8,128)(2,1)}, bf16[256,256]{1,0:T(8,128)(2,1)S(1)}, u32[]{:S(2)}, u32[]{:S(2)}) collective-permute-start(bf16[256,256]{1,0:T(8,128)(2,1)} %bitcast.5), channel_id=1, source_target_pairs={{0,8},{1,9},{2,10},{3,11},{4,12},{5,13},{6,14},{7,15},{8,0},{9,1},... | collective-permute-start | bytes 393224 | tf_op jit(solution)/shard_map/ppermute | solution.py:230
  4.7 2.5 %collective-permute-start.5 = (bf16[256,256]{1,0:T(8,128)(2,1)}, bf16[256,256]{1,0:T(8,128)(2,1)S(1)}, u32[]{:S(2)}, u32[]{:S(2)}) collective-permute-start(bf16[256,256]{1,0:T(8,128)(2,1)} %bitcast.6), channel_id=1, source_target_pairs={{0,6},{1,7},{2,4},{3,5},{4,2},{5,3},{6,0},{7,1},{8,14},{9,15},{10,... | collective-permute-start | bytes 393224 | tf_op jit(solution)/shard_map/ppermute | solution.py:230
  8.2 1.7 %shard_map.86 = (bf16[128,256]{1,0:T(8,128)(2,1)S(1)}, bf16[128,256]{1,0:T(8,128)(2,1)S(1)}, bf16[128,256]{1,0:T(8,128)(2,1)S(1)}, bf16[128,256]{1,0:T(8,128)(2,...) custom-call(s32[1]{0:T(128)} %bitcast.me_ref, ...), custom_call_target="tpu_custom_call" | custom-call | flops 1 | bytes 1 | tf_op jit(solution)/shard_map/pallas_call | solution.py:94
  9.9 1.4 %collective-permute-done.7.refs_11_.refs_12_.refs_8_ = bf16[256,256]{1,0:T(8,128)(2,1)S(1)} collective-permute-done((bf16[256,256]{1,0:T(8,128)(2,1)}, bf16[256,256]{1,0:T(8,128)(2,1)S(1)}, u32[]{:S(2)}, u32[]{:S(2)}) %collective-permute-start.7) | collective-permute-done | bytes 131104 | tf_op jit(solution)/shard_map/ppermute | solution.py:230
  11.4 2.5 %collective-permute-done.5.refs_9_.refs_10_.refs_6_ = bf16[256,256]{1,0:T(8,128)(2,1)S(1)} collective-permute-done((bf16[256,256]{1,0:T(8,128)(2,1)}, bf16[256,256]{1,0:T(8,128)(2,1)S(1)}, u32[]{:S(2)}, u32[]{:S(2)}) %collective-permute-start.5) | collective-permute-done | bytes 131104 | tf_op jit(solution)/shard_map/ppermute | solution.py:230
  13.9 1.4 %collective-permute-done.3.refs_7_.refs_8_.refs_4_ = bf16[256,256]{1,0:T(8,128)(2,1)S(1)} collective-permute-done((bf16[256,256]{1,0:T(8,128)(2,1)}, bf16[256,256]{1,0:T(8,128)(2,1)S(1)}, u32[]{:S(2)}, u32[]{:S(2)}) %collective-permute-start.3) | collective-permute-done | bytes 131104 | tf_op jit(solution)/shard_map/ppermute | solution.py:230
  15.3 1.4 %collective-permute-start.13 = (bf16[256,256]{1,0:T(8,128)(2,1)S(1)}, bf16[256,256]{1,0:T(8,128)(2,1)S(1)}, u32[]{:S(2)}, u32[]{:S(2)}) collective-permute-start(bf16[256,256]{1,0:T(8,128)(2,1)S(1)} %collective-permute-done.7.refs_11_.refs_12_.refs_8_), channel_id=1, source_target_pairs={{0,6},{1,7},{2,4},{3,5},{4,2},{5,3},{6,0},{7,1},{8,14},{9,15},{10,... | collective-permute-start | bytes 393224 | tf_op jit(solution)/shard_map/ppermute | solution.py:230
  17.3 1.5 %collective-permute-start.9 = (bf16[256,256]{1,0:T(8,128)(2,1)S(1)}, bf16[256,256]{1,0:T(8,128)(2,1)S(1)}, u32[]{:S(2)}, u32[]{:S(2)}) collective-permute-start(bf16[256,256]{1,0:T(8,128)(2,1)S(1)} %collective-permute-done.7.refs_11_.refs_12_.refs_8_), channel_id=1, source_target_pairs={{0,2},{1,3},{2,0},{3,1},{4,6},{5,7},{6,4},{7,5},{8,10},{9,11},{10,... | collective-permute-start | bytes 393224 | tf_op jit(solution)/shard_map/ppermute | solution.py:230
  19.3 2.9 %collective-permute-done.13.refs_17_.refs_18_.refs_14_ = bf16[256,256]{1,0:T(8,128)(2,1)S(1)} collective-permute-done((bf16[256,256]{1,0:T(8,128)(2,1)S(1)}, bf16[256,256]{1,0:T(8,128)(2,1)S(1)}, u32[]{:S(2)}, u32[]{:S(2)}) %collective-permute-start.13) | collective-permute-done | bytes 131104 | tf_op jit(solution)/shard_map/ppermute | solution.py:230
  26.1 1.4 %collective-permute-start.15 = (bf16[256,256]{1,0:T(8,128)(2,1)S(1)}, bf16[256,256]{1,0:T(8,128)(2,1)S(1)}, u32[]{:S(2)}, u32[]{:S(2)}) collective-permute-start(bf16[256,256]{1,0:T(8,128)(2,1)S(1)} %shard_map.87), channel_id=1, source_target_pairs={{0,8},{1,9},{2,10},{3,11},{4,12},{5,13},{6,14},{7,15},{8,0},{9,1},... | collective-permute-start | bytes 393224 | tf_op jit(solution)/shard_map/ppermute | solution.py:230
  27.5 1.2 %shard_map.88 = bf16[256,256]{1,0:T(8,128)(2,1)S(1)} custom-call(bf16[128,256]{1,0:T(8,128)(2,1)S(1)} %get-tuple-element.44.refs_0_, bf16[8,256,256]{2,1,0:T(8,128)(2,1)S(1)} %get-tuple-element.36.refs_1_.refs_2_, bf16[8,256,256]{2,1,0:T(8,128)(2,1)S(1)} %get-tuple-element.37.refs_2_.refs_3_, bf16[256,256]{1,0:T(8,128)(2,1)S(1)} %get-tuple-element.48.refs_3_.refs_4_.refs_0_, ...), custom_call_target="tpu_custom_call" | custom-call | flops 1 | bytes 1 | tf_op jit(solution)/shard_map/pallas_call | solution.py:139
  28.7 2.1 %collective-permute-start.16 = (bf16[256,256]{1,0:T(8,128)(2,1)S(1)}, bf16[256,256]{1,0:T(8,128)(2,1)S(1)}, u32[]{:S(2)}, u32[]{:S(2)}) collective-permute-start(bf16[256,256]{1,0:T(8,128)(2,1)S(1)} %shard_map.88), channel_id=1, source_target_pairs={{0,15},{1,2},{2,1},{3,4},{4,3},{5,6},{6,5},{7,8},{8,7},{9,10},{10,... | collective-permute-start | bytes 393224 | tf_op jit(solution)/shard_map/ppermute | solution.py:234
  30.8 1.8 %shard_map.89 = (bf16[256,256]{1,0:T(8,128)(2,1)S(1)}, f32[256,256]{1,0:T(8,128)S(1)}) custom-call(bf16[128,256]{1,0:T(8,128)(2,1)S(1)} %get-tuple-element.45.refs_0_, bf16[128,256]{1,0:T(8,128)(2,1)S(1)} %get-tuple-element.42.refs_1_, bf16[8,256,256]{2,1,0:T(8,128)(2,1)S(1)} %get-tuple-element.36.refs_1_.refs_2_, ...), custom_call_target="tpu_custom_call" | custom-call | flops 1 | bytes 1 | tf_op jit(solution)/shard_map/pallas_call | solution.py:139
  33.0 2.5 %collective-permute-done.15.part = bf16[256,256]{1,0:T(8,128)(2,1)S(1)} collective-permute-done((bf16[256,256]{1,0:T(8,128)(2,1)S(1)}, bf16[256,256]{1,0:T(8,128)(2,1)S(1)}, u32[]{:S(2)}, u32[]{:S(2)}) %collective-permute-start.15) | collective-permute-done | bytes 131104 | tf_op jit(solution)/shard_map/ppermute | solution.py:230
  36.0 2.6 %collective-permute-start.25 = (bf16[256,256]{1,0:T(8,128)(2,1)S(1)}, bf16[256,256]{1,0:T(8,128)(2,1)S(1)}, u32[]{:S(2)}, u32[]{:S(2)}) collective-permute-start(bf16[256,256]{1,0:T(8,128)(2,1)S(1)} %get-tuple-element.62.refs_3_.refs_4_.refs_0_), channel_id=1, source_target_pairs={{0,8},{1,9},{2,10},{3,11},{4,12},{5,13},{6,14},{7,15},{8,0},{9,1},... | collective-permute-start | bytes 393224 | tf_op jit(solution)/shard_map/ppermute | solution.py:230
  39.8 2.4 %collective-permute-start.19 = (bf16[256,256]{1,0:T(8,128)(2,1)S(1)}, bf16[256,256]{1,0:T(8,128)(2,1)S(1)}, u32[]{:S(2)}, u32[]{:S(2)}) collective-permute-start(bf16[256,256]{1,0:T(8,128)(2,1)S(1)} %get-tuple-element.62.refs_3_.refs_4_.refs_0_), channel_id=1, source_target_pairs={{0,2},{1,3},{2,0},{3,1},{4,6},{5,7},{6,4},{7,5},{8,10},{9,11},{10,... | collective-permute-start | bytes 393224 | tf_op jit(solution)/shard_map/ppermute | solution.py:230
  42.2 2.3 %collective-permute-done.25.refs_11_.refs_12_.refs_8_ = bf16[256,256]{1,0:T(8,128)(2,1)S(1)} collective-permute-done((bf16[256,256]{1,0:T(8,128)(2,1)S(1)}, bf16[256,256]{1,0:T(8,128)(2,1)S(1)}, u32[]{:S(2)}, u32[]{:S(2)}) %collective-permute-start.25) | collective-permute-done | bytes 131104 | tf_op jit(solution)/shard_map/ppermute | solution.py:230
  44.6 3.7 %collective-permute-done.23.refs_9_.refs_10_.refs_6_ = bf16[256,256]{1,0:T(8,128)(2,1)S(1)} collective-permute-done((bf16[256,256]{1,0:T(8,128)(2,1)S(1)}, bf16[256,256]{1,0:T(8,128)(2,1)S(1)}, u32[]{:S(2)}, u32[]{:S(2)}) %collective-permute-start.23) | collective-permute-done | bytes 131104 | tf_op jit(solution)/shard_map/ppermute | solution.py:230
  48.3 3.4 %collective-permute-start.27 = (bf16[256,256]{1,0:T(8,128)(2,1)S(1)}, bf16[256,256]{1,0:T(8,128)(2,1)S(1)}, u32[]{:S(2)}, u32[]{:S(2)}) collective-permute-start(bf16[256,256]{1,0:T(8,128)(2,1)S(1)} %collective-permute-done.25.refs_11_.refs_12_.refs_8_), channel_id=1, source_target_pairs={{0,2},{1,3},{2,0},{3,1},{4,6},{5,7},{6,4},{7,5},{8,10},{9,11},{10,... | collective-permute-start | bytes 393224 | tf_op jit(solution)/shard_map/ppermute | solution.py:230
  52.2 1.8 %collective-permute-done.31.refs_17_.refs_18_.refs_14_ = bf16[256,256]{1,0:T(8,128)(2,1)S(1)} collective-permute-done((bf16[256,256]{1,0:T(8,128)(2,1)S(1)}, bf16[256,256]{1,0:T(8,128)(2,1)S(1)}, u32[]{:S(2)}, u32[]{:S(2)}) %collective-permute-start.31) | collective-permute-done | bytes 131104 | tf_op jit(solution)/shard_map/ppermute | solution.py:230
  56.8 1.2 %shard_map.94 = bf16[256,256]{1,0:T(8,128)(2,1)S(1)} custom-call(bf16[128,256]{1,0:T(8,128)(2,1)S(1)} %get-tuple-element.35.refs_0_, bf16[8,256,256]{2,1,0:T(8,128)(2,1)S(1)} %get-tuple-element.36.refs_1_.refs_2_, bf16[8,256,256]{2,1,0:T(8,128)(2,1)S(1)} %get-tuple-element.37.refs_2_.refs_3_, bf16[256,256]{1,0:T(8,128)(2,1)S(1)} %get-tuple-element.62.refs_3_.refs_4_.refs_0_, ...), custom_call_target="tpu_custom_call" | custom-call | flops 1 | bytes 1 | tf_op jit(solution)/shard_map/pallas_call | solution.py:139
  59.3 2.5 %collective-permute-start.34 = (bf16[256,256]{1,0:T(8,128)(2,1)S(1)}, bf16[256,256]{1,0:T(8,128)(2,1)S(1)}, u32[]{:S(2)}, u32[]{:S(2)}) collective-permute-start(bf16[256,256]{1,0:T(8,128)(2,1)S(1)} %shard_map.95), channel_id=1, source_target_pairs={{0,15},{1,2},{2,1},{3,4},{4,3},{5,6},{6,5},{7,8},{8,7},{9,10},{10,... | collective-permute-start | bytes 393224 | tf_op jit(solution)/shard_map/ppermute | solution.py:234
  61.9 1.8 %shard_map.96 = (bf16[256,256]{1,0:T(8,128)(2,1)S(1)}, f32[256,256]{1,0:T(8,128)S(1)}) custom-call(bf16[128,256]{1,0:T(8,128)(2,1)S(1)} %get-tuple-element.53.refs_0_, bf16[128,256]{1,0:T(8,128)(2,1)S(1)} %get-tuple-element.54.refs_1_, bf16[8,256,256]{2,1,0:T(8,128)(2,1)S(1)} %get-tuple-element.36.refs_1_.refs_2_, ...), custom_call_target="tpu_custom_call" | custom-call | flops 1 | bytes 1 | tf_op jit(solution)/shard_map/pallas_call | solution.py:139
  65.4 1.9 %collective-permute-done.33.part = bf16[256,256]{1,0:T(8,128)(2,1)S(1)} collective-permute-done((bf16[256,256]{1,0:T(8,128)(2,1)S(1)}, bf16[256,256]{1,0:T(8,128)(2,1)S(1)}, u32[]{:S(2)}, u32[]{:S(2)}) %collective-permute-start.33) | collective-permute-done | bytes 131104 | tf_op jit(solution)/shard_map/ppermute | solution.py:230
  (66 shorter events, 15.1 us)
Async XLA Ops:
  0.6 10.7 %collective-permute-start.7 = (bf16[256,256]{1,0:T(8,128)(2,1)}, bf16[256,256]{1,0:T(8,128)(2,1)S(1)}, u32[]{:S(2)}, u32[]{:S(2)}) collective-permute-start(bf16[256,256]{1,0:T(8,128)(2,1)} %bitcast.5), channel_id=1, source_target_pairs={{0,8},{1,9},{2,10},{3,11},{4,12},{5,13},{6,14},{7,15},{8,0},{9,1},... | collective-permute-start | bytes 393224 | tf_op jit(solution)/shard_map/ppermute | solution.py:230
  4.7 9.2 %collective-permute-start.5 = (bf16[256,256]{1,0:T(8,128)(2,1)}, bf16[256,256]{1,0:T(8,128)(2,1)S(1)}, u32[]{:S(2)}, u32[]{:S(2)}) collective-permute-start(bf16[256,256]{1,0:T(8,128)(2,1)} %bitcast.6), channel_id=1, source_target_pairs={{0,6},{1,7},{2,4},{3,5},{4,2},{5,3},{6,0},{7,1},{8,14},{9,15},{10,... | collective-permute-start | bytes 393224 | tf_op jit(solution)/shard_map/ppermute | solution.py:230
  7.3 8.0 %collective-permute-start.3 = (bf16[256,256]{1,0:T(8,128)(2,1)}, bf16[256,256]{1,0:T(8,128)(2,1)S(1)}, u32[]{:S(2)}, u32[]{:S(2)}) collective-permute-start(bf16[256,256]{1,0:T(8,128)(2,1)} %bitcast.7), channel_id=1, source_target_pairs={{0,4},{1,5},{2,6},{3,7},{4,0},{5,1},{6,2},{7,3},{8,12},{9,13},{10,... | collective-permute-start | bytes 393224 | tf_op jit(solution)/shard_map/ppermute | solution.py:230
  7.7 9.0 %collective-permute-start.1 = (bf16[256,256]{1,0:T(8,128)(2,1)}, bf16[256,256]{1,0:T(8,128)(2,1)S(1)}, u32[]{:S(2)}, u32[]{:S(2)}) collective-permute-start(bf16[256,256]{1,0:T(8,128)(2,1)} %bitcast.8), channel_id=1, source_target_pairs={{0,2},{1,3},{2,0},{3,1},{4,6},{5,7},{6,4},{7,5},{8,10},{9,11},{10,... | collective-permute-start | bytes 393224 | tf_op jit(solution)/shard_map/ppermute | solution.py:230
  8.2 9.1 %collective-permute-start = (bf16[256,256]{1,0:T(8,128)(2,1)}, bf16[256,256]{1,0:T(8,128)(2,1)S(1)}, u32[]{:S(2)}, u32[]{:S(2)}) collective-permute-start(bf16[256,256]{1,0:T(8,128)(2,1)} %bitcast.9), channel_id=1, source_target_pairs={{0,1},{1,0},{2,3},{3,2},{4,5},{5,4},{6,7},{7,6},{8,9},{9,8},{10,11... | collective-permute-start | bytes 393224 | tf_op jit(solution)/shard_map/ppermute | solution.py:230
  11.4 7.5 %collective-permute-start.8 = (bf16[256,256]{1,0:T(8,128)(2,1)S(1)}, bf16[256,256]{1,0:T(8,128)(2,1)S(1)}, u32[]{:S(2)}, u32[]{:S(2)}) collective-permute-start(bf16[256,256]{1,0:T(8,128)(2,1)S(1)} %collective-permute-done.7.refs_11_.refs_12_.refs_8_), channel_id=1, source_target_pairs={{0,1},{1,0},{2,3},{3,2},{4,5},{5,4},{6,7},{7,6},{8,9},{9,8},{10,11... | collective-permute-start | bytes 393224 | tf_op jit(solution)/shard_map/ppermute | solution.py:230
  13.9 4.9 %collective-permute-start.6 = (bf16[256,256]{1,0:T(8,128)(2,1)S(1)}, bf16[256,256]{1,0:T(8,128)(2,1)S(1)}, u32[]{:S(2)}, u32[]{:S(2)}) collective-permute-start(bf16[256,256]{1,0:T(8,128)(2,1)S(1)} %collective-permute-done.5.refs_9_.refs_10_.refs_6_), channel_id=1, source_target_pairs={{0,1},{1,0},{2,3},{3,2},{4,5},{5,4},{6,7},{7,6},{8,9},{9,8},{10,11... | collective-permute-start | bytes 393224 | tf_op jit(solution)/shard_map/ppermute | solution.py:230
  15.3 6.9 %collective-permute-start.13 = (bf16[256,256]{1,0:T(8,128)(2,1)S(1)}, bf16[256,256]{1,0:T(8,128)(2,1)S(1)}, u32[]{:S(2)}, u32[]{:S(2)}) collective-permute-start(bf16[256,256]{1,0:T(8,128)(2,1)S(1)} %collective-permute-done.7.refs_11_.refs_12_.refs_8_), channel_id=1, source_target_pairs={{0,6},{1,7},{2,4},{3,5},{4,2},{5,3},{6,0},{7,1},{8,14},{9,15},{10,... | collective-permute-start | bytes 393224 | tf_op jit(solution)/shard_map/ppermute | solution.py:230
  16.8 6.4 %collective-permute-start.11 = (bf16[256,256]{1,0:T(8,128)(2,1)S(1)}, bf16[256,256]{1,0:T(8,128)(2,1)S(1)}, u32[]{:S(2)}, u32[]{:S(2)}) collective-permute-start(bf16[256,256]{1,0:T(8,128)(2,1)S(1)} %collective-permute-done.7.refs_11_.refs_12_.refs_8_), channel_id=1, source_target_pairs={{0,4},{1,5},{2,6},{3,7},{4,0},{5,1},{6,2},{7,3},{8,12},{9,13},{10,... | collective-permute-start | bytes 393224 | tf_op jit(solution)/shard_map/ppermute | solution.py:230
  17.3 6.2 %collective-permute-start.9 = (bf16[256,256]{1,0:T(8,128)(2,1)S(1)}, bf16[256,256]{1,0:T(8,128)(2,1)S(1)}, u32[]{:S(2)}, u32[]{:S(2)}) collective-permute-start(bf16[256,256]{1,0:T(8,128)(2,1)S(1)} %collective-permute-done.7.refs_11_.refs_12_.refs_8_), channel_id=1, source_target_pairs={{0,2},{1,3},{2,0},{3,1},{4,6},{5,7},{6,4},{7,5},{8,10},{9,11},{10,... | collective-permute-start | bytes 393224 | tf_op jit(solution)/shard_map/ppermute | solution.py:230
  18.8 4.8 %collective-permute-start.4 = (bf16[256,256]{1,0:T(8,128)(2,1)S(1)}, bf16[256,256]{1,0:T(8,128)(2,1)S(1)}, u32[]{:S(2)}, u32[]{:S(2)}) collective-permute-start(bf16[256,256]{1,0:T(8,128)(2,1)S(1)} %collective-permute-done.3.refs_7_.refs_8_.refs_4_), channel_id=1, source_target_pairs={{0,1},{1,0},{2,3},{3,2},{4,5},{5,4},{6,7},{7,6},{8,9},{9,8},{10,11... | collective-permute-start | bytes 393224 | tf_op jit(solution)/shard_map/ppermute | solution.py:230
  18.8 4.8 %collective-permute-start.2 = (bf16[256,256]{1,0:T(8,128)(2,1)S(1)}, bf16[256,256]{1,0:T(8,128)(2,1)S(1)}, u32[]{:S(2)}, u32[]{:S(2)}) collective-permute-start(bf16[256,256]{1,0:T(8,128)(2,1)S(1)} %collective-permute-done.1.refs_5_.refs_6_.refs_2_), channel_id=1, source_target_pairs={{0,1},{1,0},{2,3},{3,2},{4,5},{5,4},{6,7},{7,6},{8,9},{9,8},{10,11... | collective-permute-start | bytes 393224 | tf_op jit(solution)/shard_map/ppermute | solution.py:230
  26.1 9.4 %collective-permute-start.15 = (bf16[256,256]{1,0:T(8,128)(2,1)S(1)}, bf16[256,256]{1,0:T(8,128)(2,1)S(1)}, u32[]{:S(2)}, u32[]{:S(2)}) collective-permute-start(bf16[256,256]{1,0:T(8,128)(2,1)S(1)} %shard_map.87), channel_id=1, source_target_pairs={{0,8},{1,9},{2,10},{3,11},{4,12},{5,13},{6,14},{7,15},{8,0},{9,1},... | collective-permute-start | bytes 393224 | tf_op jit(solution)/shard_map/ppermute | solution.py:230
  28.7 7.3 %collective-permute-start.16 = (bf16[256,256]{1,0:T(8,128)(2,1)S(1)}, bf16[256,256]{1,0:T(8,128)(2,1)S(1)}, u32[]{:S(2)}, u32[]{:S(2)}) collective-permute-start(bf16[256,256]{1,0:T(8,128)(2,1)S(1)} %shard_map.88), channel_id=1, source_target_pairs={{0,15},{1,2},{2,1},{3,4},{4,3},{5,6},{6,5},{7,8},{8,7},{9,10},{10,... | collective-permute-start | bytes 393224 | tf_op jit(solution)/shard_map/ppermute | solution.py:234
  36.0 8.4 %collective-permute-start.25 = (bf16[256,256]{1,0:T(8,128)(2,1)S(1)}, bf16[256,256]{1,0:T(8,128)(2,1)S(1)}, u32[]{:S(2)}, u32[]{:S(2)}) collective-permute-start(bf16[256,256]{1,0:T(8,128)(2,1)S(1)} %get-tuple-element.62.refs_3_.refs_4_.refs_0_), channel_id=1, source_target_pairs={{0,8},{1,9},{2,10},{3,11},{4,12},{5,13},{6,14},{7,15},{8,0},{9,1},... | collective-permute-start | bytes 393224 | tf_op jit(solution)/shard_map/ppermute | solution.py:230
  38.7 9.6 %collective-permute-start.23 = (bf16[256,256]{1,0:T(8,128)(2,1)S(1)}, bf16[256,256]{1,0:T(8,128)(2,1)S(1)}, u32[]{:S(2)}, u32[]{:S(2)}) collective-permute-start(bf16[256,256]{1,0:T(8,128)(2,1)S(1)} %get-tuple-element.62.refs_3_.refs_4_.refs_0_), channel_id=1, source_target_pairs={{0,6},{1,7},{2,4},{3,5},{4,2},{5,3},{6,0},{7,1},{8,14},{9,15},{10,... | collective-permute-start | bytes 393224 | tf_op jit(solution)/shard_map/ppermute | solution.py:230
  38.8 9.4 %collective-permute-start.21 = (bf16[256,256]{1,0:T(8,128)(2,1)S(1)}, bf16[256,256]{1,0:T(8,128)(2,1)S(1)}, u32[]{:S(2)}, u32[]{:S(2)}) collective-permute-start(bf16[256,256]{1,0:T(8,128)(2,1)S(1)} %get-tuple-element.62.refs_3_.refs_4_.refs_0_), channel_id=1, source_target_pairs={{0,4},{1,5},{2,6},{3,7},{4,0},{5,1},{6,2},{7,3},{8,12},{9,13},{10,... | collective-permute-start | bytes 393224 | tf_op jit(solution)/shard_map/ppermute | solution.py:230
  39.8 11.9 %collective-permute-start.19 = (bf16[256,256]{1,0:T(8,128)(2,1)S(1)}, bf16[256,256]{1,0:T(8,128)(2,1)S(1)}, u32[]{:S(2)}, u32[]{:S(2)}) collective-permute-start(bf16[256,256]{1,0:T(8,128)(2,1)S(1)} %get-tuple-element.62.refs_3_.refs_4_.refs_0_), channel_id=1, source_target_pairs={{0,2},{1,3},{2,0},{3,1},{4,6},{5,7},{6,4},{7,5},{8,10},{9,11},{10,... | collective-permute-start | bytes 393224 | tf_op jit(solution)/shard_map/ppermute | solution.py:230
  42.2 9.5 %collective-permute-start.18 = (bf16[256,256]{1,0:T(8,128)(2,1)S(1)}, bf16[256,256]{1,0:T(8,128)(2,1)S(1)}, u32[]{:S(2)}, u32[]{:S(2)}) collective-permute-start(bf16[256,256]{1,0:T(8,128)(2,1)S(1)} %get-tuple-element.62.refs_3_.refs_4_.refs_0_), channel_id=1, source_target_pairs={{0,1},{1,0},{2,3},{3,2},{4,5},{5,4},{6,7},{7,6},{8,9},{9,8},{10,11... | collective-permute-start | bytes 393224 | tf_op jit(solution)/shard_map/ppermute | solution.py:230
  44.4 9.5 %collective-permute-start.31 = (bf16[256,256]{1,0:T(8,128)(2,1)S(1)}, bf16[256,256]{1,0:T(8,128)(2,1)S(1)}, u32[]{:S(2)}, u32[]{:S(2)}) collective-permute-start(bf16[256,256]{1,0:T(8,128)(2,1)S(1)} %collective-permute-done.25.refs_11_.refs_12_.refs_8_), channel_id=1, source_target_pairs={{0,6},{1,7},{2,4},{3,5},{4,2},{5,3},{6,0},{7,1},{8,14},{9,15},{10,... | collective-permute-start | bytes 393224 | tf_op jit(solution)/shard_map/ppermute | solution.py:230
  48.3 5.7 %collective-permute-start.29 = (bf16[256,256]{1,0:T(8,128)(2,1)S(1)}, bf16[256,256]{1,0:T(8,128)(2,1)S(1)}, u32[]{:S(2)}, u32[]{:S(2)}) collective-permute-start(bf16[256,256]{1,0:T(8,128)(2,1)S(1)} %collective-permute-done.25.refs_11_.refs_12_.refs_8_), channel_id=1, source_target_pairs={{0,4},{1,5},{2,6},{3,7},{4,0},{5,1},{6,2},{7,3},{8,12},{9,13},{10,... | collective-permute-start | bytes 393224 | tf_op jit(solution)/shard_map/ppermute | solution.py:230
  48.3 6.7 %collective-permute-start.27 = (bf16[256,256]{1,0:T(8,128)(2,1)S(1)}, bf16[256,256]{1,0:T(8,128)(2,1)S(1)}, u32[]{:S(2)}, u32[]{:S(2)}) collective-permute-start(bf16[256,256]{1,0:T(8,128)(2,1)S(1)} %collective-permute-done.25.refs_11_.refs_12_.refs_8_), channel_id=1, source_target_pairs={{0,2},{1,3},{2,0},{3,1},{4,6},{5,7},{6,4},{7,5},{8,10},{9,11},{10,... | collective-permute-start | bytes 393224 | tf_op jit(solution)/shard_map/ppermute | solution.py:230
  58.0 9.2 %collective-permute-start.33 = (bf16[256,256]{1,0:T(8,128)(2,1)S(1)}, bf16[256,256]{1,0:T(8,128)(2,1)S(1)}, u32[]{:S(2)}, u32[]{:S(2)}) collective-permute-start(bf16[256,256]{1,0:T(8,128)(2,1)S(1)} %shard_map.94), channel_id=1, source_target_pairs={{0,8},{1,9},{2,10},{3,11},{4,12},{5,13},{6,14},{7,15},{8,0},{9,1},... | collective-permute-start | bytes 393224 | tf_op jit(solution)/shard_map/ppermute | solution.py:230
  59.3 7.9 %collective-permute-start.34 = (bf16[256,256]{1,0:T(8,128)(2,1)S(1)}, bf16[256,256]{1,0:T(8,128)(2,1)S(1)}, u32[]{:S(2)}, u32[]{:S(2)}) collective-permute-start(bf16[256,256]{1,0:T(8,128)(2,1)S(1)} %shard_map.95), channel_id=1, source_target_pairs={{0,15},{1,2},{2,1},{3,4},{4,3},{5,6},{6,5},{7,8},{8,7},{9,10},{10,... | collective-permute-start | bytes 393224 | tf_op jit(solution)/shard_map/ppermute | solution.py:234
  (13 other events, 28.2 us)
where the time goes:
time: 68.2 us; the launch traced here: 68.1 us
  starting transfers between devices  29.3 us (43%)
  waiting for transfers between devices  25.1 us (37%)
  Pallas kernels  12.8 us (19%)
  between operations  0.81 us (1%)
    ppermute x34, waiting for transfers between devices, swap(): return lax.ppermute(x, 'op', [(i, i ^ mask) for i in range(count)])  24.7 us
    ppermute x34, starting transfers between devices, swap(): return lax.ppermute(x, 'op', [(i, i ^ mask) for i in range(count)])  24.6 us
    pallas_call x6, Pallas kernels, sums(): pl.pallas_call(functools.partial(sums_body, count, slots), out_shape=[plt...  8.4 us
    ppermute x2, starting transfers between devices, swap_other(): lax.ppermute(x, 'op', [(i, (i + (1 if i % 2 else count - 1)) % count) for...  4.66 us
    pallas_call x8, Pallas kernels, small(): pl.pallas_call(body, out_shape=shapes, in_specs=spec(len(inputs)), out_sp...  1.87 us
    pallas_call x1, Pallas kernels, prepare(): pl.pallas_call(functools.partial(prepare_body, count), out_shape=[pltpu.V...  1.71 us
  transfers between devices with their start and end apart: 36, of which 18 were waited for; matrix products, arithmetic and copies ran while one was open for 0% of the time, Pallas kernels for 14%

commit v1 on v0

--- a/solution.py
+++ b/solution.py
@@ -129,9 +129,16 @@
         outs[t][...] = total.astype(outs[t].dtype)
 
 
+def operand_order(count):
+    near = sorted(range(2, count // 2, 2), key=lambda m: -m.bit_count())
+    return [m + c for m in (0, *near, *range(count // 2, count, 2)) for c in (0, 1)]
+
+
 def sums_body(count, slots, *refs):
     w_refs, (left_ref, right_ref), refs = refs[:slots], refs[slots : slots + 2], refs[slots + 2 :]
-    products(w_refs, left_ref, right_ref, refs[:count], refs[count:-2], *refs[-2:])
+    order = operand_order(count)
+    blocks = [refs[order.index(m)] for m in range(count)]
+    products(w_refs, left_ref, right_ref, blocks, refs[count:-2], *refs[-2:])
 
 
 def sums(weights, left_ops, right_ops, blocks, types):
@@ -147,7 +154,7 @@
         ],
         cost_estimate=cost(1),
         compiler_params=params(12),
-    )(*[in_vmem(x) for x in (*weights, left_ops, right_ops, *blocks)])
+    )(*[in_vmem(x) for x in (*weights, left_ops, right_ops, *[blocks[m] for m in operand_order(count)])])
 
 
 def small(body, shapes, inputs, flops=1):
@@ -240,8 +247,8 @@
     for mask in range(2, half, 2):
         blocks[mask] = swap(field, count, mask)
     blocks[half] = swap(field, count, half)
-    far = after(blocks[half], *prepared) if prepared else blocks[half]
     for mask in range(2, half, 2):
+        far = after(blocks[half], *prepared) if prepared and mask == 2 else blocks[half]
         blocks[half + mask] = swap(far, count, mask)
     for mask in range(0, count, 2):
         blocks[mask + 1] = swap(blocks[mask], count, 1)

time: 68.2 us -> 66.1 us (0.969)
  starting transfers between devices: 29.3 us -> 28.1 us
  waiting for transfers between devices: 25.1 us -> 24.2 us
    ppermute x34, starting transfers between devices: 24.6 us -> 23.1 us  [swap(): return lax.ppermute(x, 'op', [(i, i ^ mask) for i in range(count)])]
  transfers between devices with their start and end apart: 36 -> 36, of which waited for: 18 -> 19; matrix products, arithmetic and copies ran while one was open for 0% -> 0% of each run, Pallas kernels for 14% -> 15%
where the time goes in v1:
time: 66.1 us; the launch traced here: 66 us
  starting transfers between devices  28.1 us (43%)
  waiting for transfers between devices  24.2 us (37%)
  Pallas kernels  12.8 us (19%)
  between operations  0.83 us (1%)
    ppermute x34, waiting for transfers between devices, swap(): return lax.ppermute(x, 'op', [(i, i ^ mask) for i in range(count)])  24.1 us
    ppermute x34, starting transfers between devices, swap(): return lax.ppermute(x, 'op', [(i, i ^ mask) for i in range(count)])  23.1 us
    pallas_call x6, Pallas kernels, sums(): pl.pallas_call(functools.partial(sums_body, count, slots), out_shape=[plt...  8.4 us
    ppermute x2, starting transfers between devices, swap_other(): lax.ppermute(x, 'op', [(i, (i + (1 if i % 2 else count - 1)) % count) for...  4.94 us
    pallas_call x8, Pallas kernels, small(): pl.pallas_call(body, out_shape=shapes, in_specs=spec(len(inputs)), out_sp...  1.87 us
    pallas_call x1, Pallas kernels, prepare(): pl.pallas_call(functools.partial(prepare_body, count), out_shape=[pltpu.V...  1.71 us
  transfers between devices with their start and end apart: 36, of which 19 were waited for; matrix products, arithmetic and copies ran while one was open for 0% of the time, Pallas kernels for 15%

profile of v1, /device:TPU:0, one launch (start us, length us, event | category | flops | bytes accessed | tf_op | source)
XLA Modules:
  0.0 66.0 jit_solution(5920614537267044586)
XLA Ops:
  0.6 4.1 %collective-permute-start.7 = (bf16[256,256]{1,0:T(8,128)(2,1)}, bf16[256,256]{1,0:T(8,128)(2,1)S(1)}, u32[]{:S(2)}, u32[]{:S(2)}) collective-permute-start(bf16[256,256]{1,0:T(8,128)(2,1)} %bitcast.5), channel_id=1, source_target_pairs={{0,8},{1,9},{2,10},{3,11},{4,12},{5,13},{6,14},{7,15},{8,0},{9,1},... | collective-permute-start | bytes 393224 | tf_op jit(solution)/shard_map/ppermute | solution.py:237
  4.7 1.6 %collective-permute-start.5 = (bf16[256,256]{1,0:T(8,128)(2,1)}, bf16[256,256]{1,0:T(8,128)(2,1)S(1)}, u32[]{:S(2)}, u32[]{:S(2)}) collective-permute-start(bf16[256,256]{1,0:T(8,128)(2,1)} %bitcast.6), channel_id=1, source_target_pairs={{0,4},{1,5},{2,6},{3,7},{4,0},{5,1},{6,2},{7,3},{8,12},{9,13},{10,... | collective-permute-start | bytes 393224 | tf_op jit(solution)/shard_map/ppermute | solution.py:237
  6.3 1.5 %collective-permute-start.3 = (bf16[256,256]{1,0:T(8,128)(2,1)}, bf16[256,256]{1,0:T(8,128)(2,1)S(1)}, u32[]{:S(2)}, u32[]{:S(2)}) collective-permute-start(bf16[256,256]{1,0:T(8,128)(2,1)} %bitcast.7), channel_id=1, source_target_pairs={{0,2},{1,3},{2,0},{3,1},{4,6},{5,7},{6,4},{7,5},{8,10},{9,11},{10,... | collective-permute-start | bytes 393224 | tf_op jit(solution)/shard_map/ppermute | solution.py:237
  8.2 1.7 %shard_map.86 = (bf16[128,256]{1,0:T(8,128)(2,1)S(1)}, bf16[128,256]{1,0:T(8,128)(2,1)S(1)}, bf16[128,256]{1,0:T(8,128)(2,1)S(1)}, bf16[128,256]{1,0:T(8,128)(2,...) custom-call(s32[1]{0:T(128)} %bitcast.me_ref, ...), custom_call_target="tpu_custom_call" | custom-call | flops 1 | bytes 1 | tf_op jit(solution)/shard_map/pallas_call | solution.py:94
  9.9 1.4 %collective-permute-done.7.refs_11_.refs_12_.refs_8_ = bf16[256,256]{1,0:T(8,128)(2,1)S(1)} collective-permute-done((bf16[256,256]{1,0:T(8,128)(2,1)}, bf16[256,256]{1,0:T(8,128)(2,1)S(1)}, u32[]{:S(2)}, u32[]{:S(2)}) %collective-permute-start.7) | collective-permute-done | bytes 131104 | tf_op jit(solution)/shard_map/ppermute | solution.py:237
  11.3 1.7 %collective-permute-start.13 = (bf16[256,256]{1,0:T(8,128)(2,1)S(1)}, bf16[256,256]{1,0:T(8,128)(2,1)S(1)}, u32[]{:S(2)}, u32[]{:S(2)}) collective-permute-start(bf16[256,256]{1,0:T(8,128)(2,1)S(1)} %collective-permute-done.7.refs_11_.refs_12_.refs_8_), channel_id=1, source_target_pairs={{0,6},{1,7},{2,4},{3,5},{4,2},{5,3},{6,0},{7,1},{8,14},{9,15},{10,... | collective-permute-start | bytes 393224 | tf_op jit(solution)/shard_map/ppermute | solution.py:237
  13.1 1.3 %collective-permute-start.11 = (bf16[256,256]{1,0:T(8,128)(2,1)S(1)}, bf16[256,256]{1,0:T(8,128)(2,1)S(1)}, u32[]{:S(2)}, u32[]{:S(2)}) collective-permute-start(bf16[256,256]{1,0:T(8,128)(2,1)S(1)} %collective-permute-done.7.refs_11_.refs_12_.refs_8_), channel_id=1, source_target_pairs={{0,4},{1,5},{2,6},{3,7},{4,0},{5,1},{6,2},{7,3},{8,12},{9,13},{10,... | collective-permute-start | bytes 393224 | tf_op jit(solution)/shard_map/ppermute | solution.py:237
  14.4 1.8 %collective-permute-done.1.refs_5_.refs_6_ = bf16[256,256]{1,0:T(8,128)(2,1)S(1)} collective-permute-done((bf16[256,256]{1,0:T(8,128)(2,1)}, bf16[256,256]{1,0:T(8,128)(2,1)S(1)}, u32[]{:S(2)}, u32[]{:S(2)}) %collective-permute-start.1) | collective-permute-done | bytes 131104 | tf_op jit(solution)/shard_map/ppermute | solution.py:237
  16.2 2.8 %collective-permute-done.13.refs_17_.refs_18_.refs_14_ = bf16[256,256]{1,0:T(8,128)(2,1)S(1)} collective-permute-done((bf16[256,256]{1,0:T(8,128)(2,1)S(1)}, bf16[256,256]{1,0:T(8,128)(2,1)S(1)}, u32[]{:S(2)}, u32[]{:S(2)}) %collective-permute-start.13) | collective-permute-done | bytes 131104 | tf_op jit(solution)/shard_map/ppermute | solution.py:237
  20.6 1.6 %collective-permute-done.9.refs_13_.refs_14_.refs_10_ = bf16[256,256]{1,0:T(8,128)(2,1)S(1)} collective-permute-done((bf16[256,256]{1,0:T(8,128)(2,1)S(1)}, bf16[256,256]{1,0:T(8,128)(2,1)S(1)}, u32[]{:S(2)}, u32[]{:S(2)}) %collective-permute-start.9) | collective-permute-done | bytes 131104 | tf_op jit(solution)/shard_map/ppermute | solution.py:237
  22.2 1.3 %collective-permute-done.10.refs_14_.refs_15_.refs_11_ = bf16[256,256]{1,0:T(8,128)(2,1)S(1)} collective-permute-done((bf16[256,256]{1,0:T(8,128)(2,1)S(1)}, bf16[256,256]{1,0:T(8,128)(2,1)S(1)}, u32[]{:S(2)}, u32[]{:S(2)}) %collective-permute-start.10) | collective-permute-done | bytes 131104 | tf_op jit(solution)/shard_map/ppermute | solution.py:237
  26.9 2.3 %collective-permute-start.16 = (bf16[256,256]{1,0:T(8,128)(2,1)S(1)}, bf16[256,256]{1,0:T(8,128)(2,1)S(1)}, u32[]{:S(2)}, u32[]{:S(2)}) collective-permute-start(bf16[256,256]{1,0:T(8,128)(2,1)S(1)} %shard_map.88), channel_id=1, source_target_pairs={{0,15},{1,2},{2,1},{3,4},{4,3},{5,6},{6,5},{7,8},{8,7},{9,10},{10,... | collective-permute-start | bytes 393224 | tf_op jit(solution)/shard_map/ppermute | solution.py:241
  29.2 1.8 %shard_map.89 = (bf16[256,256]{1,0:T(8,128)(2,1)S(1)}, f32[256,256]{1,0:T(8,128)S(1)}) custom-call(bf16[128,256]{1,0:T(8,128)(2,1)S(1)} %get-tuple-element.45.refs_0_, bf16[128,256]{1,0:T(8,128)(2,1)S(1)} %get-tuple-element.42.refs_1_, bf16[8,256,256]{2,1,0:T(8,128)(2,1)S(1)} %get-tuple-element.36.refs_1_.refs_2_, ...), custom_call_target="tpu_custom_call" | custom-call | flops 1 | bytes 1 | tf_op jit(solution)/shard_map/pallas_call | solution.py:146
  31.3 2.7 %collective-permute-done.15.part = bf16[256,256]{1,0:T(8,128)(2,1)S(1)} collective-permute-done((bf16[256,256]{1,0:T(8,128)(2,1)S(1)}, bf16[256,256]{1,0:T(8,128)(2,1)S(1)}, u32[]{:S(2)}, u32[]{:S(2)}) %collective-permute-start.15) | collective-permute-done | bytes 131104 | tf_op jit(solution)/shard_map/ppermute | solution.py:237
  34.2 3.0 %collective-permute-start.25 = (bf16[256,256]{1,0:T(8,128)(2,1)S(1)}, bf16[256,256]{1,0:T(8,128)(2,1)S(1)}, u32[]{:S(2)}, u32[]{:S(2)}) collective-permute-start(bf16[256,256]{1,0:T(8,128)(2,1)S(1)} %get-tuple-element.62.refs_3_.refs_4_.refs_0_), channel_id=1, source_target_pairs={{0,8},{1,9},{2,10},{3,11},{4,12},{5,13},{6,14},{7,15},{8,0},{9,1},... | collective-permute-start | bytes 393224 | tf_op jit(solution)/shard_map/ppermute | solution.py:237
  37.2 1.4 %collective-permute-start.23 = (bf16[256,256]{1,0:T(8,128)(2,1)S(1)}, bf16[256,256]{1,0:T(8,128)(2,1)S(1)}, u32[]{:S(2)}, u32[]{:S(2)}) collective-permute-start(bf16[256,256]{1,0:T(8,128)(2,1)S(1)} %get-tuple-element.62.refs_3_.refs_4_.refs_0_), channel_id=1, source_target_pairs={{0,4},{1,5},{2,6},{3,7},{4,0},{5,1},{6,2},{7,3},{8,12},{9,13},{10,... | collective-permute-start | bytes 393224 | tf_op jit(solution)/shard_map/ppermute | solution.py:237
  38.6 2.1 %collective-permute-start.19 = (bf16[256,256]{1,0:T(8,128)(2,1)S(1)}, bf16[256,256]{1,0:T(8,128)(2,1)S(1)}, u32[]{:S(2)}, u32[]{:S(2)}) collective-permute-start(bf16[256,256]{1,0:T(8,128)(2,1)S(1)} %get-tuple-element.62.refs_3_.refs_4_.refs_0_), channel_id=1, source_target_pairs={{0,6},{1,7},{2,4},{3,5},{4,2},{5,3},{6,0},{7,1},{8,14},{9,15},{10,... | collective-permute-start | bytes 393224 | tf_op jit(solution)/shard_map/ppermute | solution.py:237
  40.7 2.0 %collective-permute-done.25.refs_11_.refs_12_.refs_8_ = bf16[256,256]{1,0:T(8,128)(2,1)S(1)} collective-permute-done((bf16[256,256]{1,0:T(8,128)(2,1)S(1)}, bf16[256,256]{1,0:T(8,128)(2,1)S(1)}, u32[]{:S(2)}, u32[]{:S(2)}) %collective-permute-start.25) | collective-permute-done | bytes 131104 | tf_op jit(solution)/shard_map/ppermute | solution.py:237
  44.3 2.0 %collective-permute-start.29 = (bf16[256,256]{1,0:T(8,128)(2,1)S(1)}, bf16[256,256]{1,0:T(8,128)(2,1)S(1)}, u32[]{:S(2)}, u32[]{:S(2)}) collective-permute-start(bf16[256,256]{1,0:T(8,128)(2,1)S(1)} %collective-permute-done.25.refs_11_.refs_12_.refs_8_), channel_id=1, source_target_pairs={{0,4},{1,5},{2,6},{3,7},{4,0},{5,1},{6,2},{7,3},{8,12},{9,13},{10,... | collective-permute-start | bytes 393224 | tf_op jit(solution)/shard_map/ppermute | solution.py:237
  47.9 2.3 %collective-permute-done.31.refs_17_.refs_18_.refs_14_ = bf16[256,256]{1,0:T(8,128)(2,1)S(1)} collective-permute-done((bf16[256,256]{1,0:T(8,128)(2,1)S(1)}, bf16[256,256]{1,0:T(8,128)(2,1)S(1)}, u32[]{:S(2)}, u32[]{:S(2)}) %collective-permute-start.31) | collective-permute-done | bytes 131104 | tf_op jit(solution)/shard_map/ppermute | solution.py:237
  50.2 2.0 %collective-permute-done.29.refs_15_.refs_16_.refs_12_ = bf16[256,256]{1,0:T(8,128)(2,1)S(1)} collective-permute-done((bf16[256,256]{1,0:T(8,128)(2,1)S(1)}, bf16[256,256]{1,0:T(8,128)(2,1)S(1)}, u32[]{:S(2)}, u32[]{:S(2)}) %collective-permute-start.29) | collective-permute-done | bytes 131104 | tf_op jit(solution)/shard_map/ppermute | solution.py:237
  57.5 2.7 %collective-permute-start.34 = (bf16[256,256]{1,0:T(8,128)(2,1)S(1)}, bf16[256,256]{1,0:T(8,128)(2,1)S(1)}, u32[]{:S(2)}, u32[]{:S(2)}) collective-permute-start(bf16[256,256]{1,0:T(8,128)(2,1)S(1)} %shard_map.95), channel_id=1, source_target_pairs={{0,15},{1,2},{2,1},{3,4},{4,3},{5,6},{6,5},{7,8},{8,7},{9,10},{10,... | collective-permute-start | bytes 393224 | tf_op jit(solution)/shard_map/ppermute | solution.py:241
  60.2 1.8 %shard_map.96 = (bf16[256,256]{1,0:T(8,128)(2,1)S(1)}, f32[256,256]{1,0:T(8,128)S(1)}) custom-call(bf16[128,256]{1,0:T(8,128)(2,1)S(1)} %get-tuple-element.53.refs_0_, bf16[128,256]{1,0:T(8,128)(2,1)S(1)} %get-tuple-element.54.refs_1_, bf16[8,256,256]{2,1,0:T(8,128)(2,1)S(1)} %get-tuple-element.36.refs_1_.refs_2_, ...), custom_call_target="tpu_custom_call" | custom-call | flops 1 | bytes 1 | tf_op jit(solution)/shard_map/pallas_call | solution.py:146
  63.7 1.5 %collective-permute-done.33.part = bf16[256,256]{1,0:T(8,128)(2,1)S(1)} collective-permute-done((bf16[256,256]{1,0:T(8,128)(2,1)S(1)}, bf16[256,256]{1,0:T(8,128)(2,1)S(1)}, u32[]{:S(2)}, u32[]{:S(2)}) %collective-permute-start.33) | collective-permute-done | bytes 131104 | tf_op jit(solution)/shard_map/ppermute | solution.py:237
  (66 shorter events, 16.8 us)
Async XLA Ops:
  0.6 10.7 %collective-permute-start.7 = (bf16[256,256]{1,0:T(8,128)(2,1)}, bf16[256,256]{1,0:T(8,128)(2,1)S(1)}, u32[]{:S(2)}, u32[]{:S(2)}) collective-permute-start(bf16[256,256]{1,0:T(8,128)(2,1)} %bitcast.5), channel_id=1, source_target_pairs={{0,8},{1,9},{2,10},{3,11},{4,12},{5,13},{6,14},{7,15},{8,0},{9,1},... | collective-permute-start | bytes 393224 | tf_op jit(solution)/shard_map/ppermute | solution.py:237
  4.7 8.3 %collective-permute-start.5 = (bf16[256,256]{1,0:T(8,128)(2,1)}, bf16[256,256]{1,0:T(8,128)(2,1)S(1)}, u32[]{:S(2)}, u32[]{:S(2)}) collective-permute-start(bf16[256,256]{1,0:T(8,128)(2,1)} %bitcast.6), channel_id=1, source_target_pairs={{0,4},{1,5},{2,6},{3,7},{4,0},{5,1},{6,2},{7,3},{8,12},{9,13},{10,... | collective-permute-start | bytes 393224 | tf_op jit(solution)/shard_map/ppermute | solution.py:237
  6.3 8.1 %collective-permute-start.3 = (bf16[256,256]{1,0:T(8,128)(2,1)}, bf16[256,256]{1,0:T(8,128)(2,1)S(1)}, u32[]{:S(2)}, u32[]{:S(2)}) collective-permute-start(bf16[256,256]{1,0:T(8,128)(2,1)} %bitcast.7), channel_id=1, source_target_pairs={{0,2},{1,3},{2,0},{3,1},{4,6},{5,7},{6,4},{7,5},{8,10},{9,11},{10,... | collective-permute-start | bytes 393224 | tf_op jit(solution)/shard_map/ppermute | solution.py:237
  7.8 8.4 %collective-permute-start.1 = (bf16[256,256]{1,0:T(8,128)(2,1)}, bf16[256,256]{1,0:T(8,128)(2,1)S(1)}, u32[]{:S(2)}, u32[]{:S(2)}) collective-permute-start(bf16[256,256]{1,0:T(8,128)(2,1)} %bitcast.8), channel_id=1, source_target_pairs={{0,6},{1,7},{2,4},{3,5},{4,2},{5,3},{6,0},{7,1},{8,14},{9,15},{10,... | collective-permute-start | bytes 393224 | tf_op jit(solution)/shard_map/ppermute | solution.py:237
  8.2 8.0 %collective-permute-start = (bf16[256,256]{1,0:T(8,128)(2,1)}, bf16[256,256]{1,0:T(8,128)(2,1)S(1)}, u32[]{:S(2)}, u32[]{:S(2)}) collective-permute-start(bf16[256,256]{1,0:T(8,128)(2,1)} %bitcast.9), channel_id=1, source_target_pairs={{0,1},{1,0},{2,3},{3,2},{4,5},{5,4},{6,7},{7,6},{8,9},{9,8},{10,11... | collective-permute-start | bytes 393224 | tf_op jit(solution)/shard_map/ppermute | solution.py:237
  11.3 7.7 %collective-permute-start.13 = (bf16[256,256]{1,0:T(8,128)(2,1)S(1)}, bf16[256,256]{1,0:T(8,128)(2,1)S(1)}, u32[]{:S(2)}, u32[]{:S(2)}) collective-permute-start(bf16[256,256]{1,0:T(8,128)(2,1)S(1)} %collective-permute-done.7.refs_11_.refs_12_.refs_8_), channel_id=1, source_target_pairs={{0,6},{1,7},{2,4},{3,5},{4,2},{5,3},{6,0},{7,1},{8,14},{9,15},{10,... | collective-permute-start | bytes 393224 | tf_op jit(solution)/shard_map/ppermute | solution.py:237
  13.1 6.9 %collective-permute-start.11 = (bf16[256,256]{1,0:T(8,128)(2,1)S(1)}, bf16[256,256]{1,0:T(8,128)(2,1)S(1)}, u32[]{:S(2)}, u32[]{:S(2)}) collective-permute-start(bf16[256,256]{1,0:T(8,128)(2,1)S(1)} %collective-permute-done.7.refs_11_.refs_12_.refs_8_), channel_id=1, source_target_pairs={{0,4},{1,5},{2,6},{3,7},{4,0},{5,1},{6,2},{7,3},{8,12},{9,13},{10,... | collective-permute-start | bytes 393224 | tf_op jit(solution)/shard_map/ppermute | solution.py:237
  14.4 5.6 %collective-permute-start.8 = (bf16[256,256]{1,0:T(8,128)(2,1)S(1)}, bf16[256,256]{1,0:T(8,128)(2,1)S(1)}, u32[]{:S(2)}, u32[]{:S(2)}) collective-permute-start(bf16[256,256]{1,0:T(8,128)(2,1)S(1)} %collective-permute-done.7.refs_11_.refs_12_.refs_8_), channel_id=1, source_target_pairs={{0,1},{1,0},{2,3},{3,2},{4,5},{5,4},{6,7},{7,6},{8,9},{9,8},{10,11... | collective-permute-start | bytes 393224 | tf_op jit(solution)/shard_map/ppermute | solution.py:237
  16.2 4.3 %collective-permute-start.6 = (bf16[256,256]{1,0:T(8,128)(2,1)S(1)}, bf16[256,256]{1,0:T(8,128)(2,1)S(1)}, u32[]{:S(2)}, u32[]{:S(2)}) collective-permute-start(bf16[256,256]{1,0:T(8,128)(2,1)S(1)} %collective-permute-done.5.refs_9_.refs_10_.refs_4_), channel_id=1, source_target_pairs={{0,1},{1,0},{2,3},{3,2},{4,5},{5,4},{6,7},{7,6},{8,9},{9,8},{10,11... | collective-permute-start | bytes 393224 | tf_op jit(solution)/shard_map/ppermute | solution.py:237
  16.2 5.9 %collective-permute-start.9 = (bf16[256,256]{1,0:T(8,128)(2,1)S(1)}, bf16[256,256]{1,0:T(8,128)(2,1)S(1)}, u32[]{:S(2)}, u32[]{:S(2)}) collective-permute-start(bf16[256,256]{1,0:T(8,128)(2,1)S(1)} %collective-permute-done.7.refs_11_.refs_12_.refs_8_), channel_id=1, source_target_pairs={{0,2},{1,3},{2,0},{3,1},{4,6},{5,7},{6,4},{7,5},{8,10},{9,11},{10,... | collective-permute-start | bytes 393224 | tf_op jit(solution)/shard_map/ppermute | solution.py:237
  24.7 9.3 %collective-permute-start.15 = (bf16[256,256]{1,0:T(8,128)(2,1)S(1)}, bf16[256,256]{1,0:T(8,128)(2,1)S(1)}, u32[]{:S(2)}, u32[]{:S(2)}) collective-permute-start(bf16[256,256]{1,0:T(8,128)(2,1)S(1)} %shard_map.87), channel_id=1, source_target_pairs={{0,8},{1,9},{2,10},{3,11},{4,12},{5,13},{6,14},{7,15},{8,0},{9,1},... | collective-permute-start | bytes 393224 | tf_op jit(solution)/shard_map/ppermute | solution.py:237
  26.9 7.3 %collective-permute-start.16 = (bf16[256,256]{1,0:T(8,128)(2,1)S(1)}, bf16[256,256]{1,0:T(8,128)(2,1)S(1)}, u32[]{:S(2)}, u32[]{:S(2)}) collective-permute-start(bf16[256,256]{1,0:T(8,128)(2,1)S(1)} %shard_map.88), channel_id=1, source_target_pairs={{0,15},{1,2},{2,1},{3,4},{4,3},{5,6},{6,5},{7,8},{8,7},{9,10},{10,... | collective-permute-start | bytes 393224 | tf_op jit(solution)/shard_map/ppermute | solution.py:241
  34.2 8.5 %collective-permute-start.25 = (bf16[256,256]{1,0:T(8,128)(2,1)S(1)}, bf16[256,256]{1,0:T(8,128)(2,1)S(1)}, u32[]{:S(2)}, u32[]{:S(2)}) collective-permute-start(bf16[256,256]{1,0:T(8,128)(2,1)S(1)} %get-tuple-element.62.refs_3_.refs_4_.refs_0_), channel_id=1, source_target_pairs={{0,8},{1,9},{2,10},{3,11},{4,12},{5,13},{6,14},{7,15},{8,0},{9,1},... | collective-permute-start | bytes 393224 | tf_op jit(solution)/shard_map/ppermute | solution.py:237
  37.2 7.1 %collective-permute-start.23 = (bf16[256,256]{1,0:T(8,128)(2,1)S(1)}, bf16[256,256]{1,0:T(8,128)(2,1)S(1)}, u32[]{:S(2)}, u32[]{:S(2)}) collective-permute-start(bf16[256,256]{1,0:T(8,128)(2,1)S(1)} %get-tuple-element.62.refs_3_.refs_4_.refs_0_), channel_id=1, source_target_pairs={{0,4},{1,5},{2,6},{3,7},{4,0},{5,1},{6,2},{7,3},{8,12},{9,13},{10,... | collective-permute-start | bytes 393224 | tf_op jit(solution)/shard_map/ppermute | solution.py:237
  38.6 7.7 %collective-permute-start.21 = (bf16[256,256]{1,0:T(8,128)(2,1)S(1)}, bf16[256,256]{1,0:T(8,128)(2,1)S(1)}, u32[]{:S(2)}, u32[]{:S(2)}) collective-permute-start(bf16[256,256]{1,0:T(8,128)(2,1)S(1)} %get-tuple-element.62.refs_3_.refs_4_.refs_0_), channel_id=1, source_target_pairs={{0,2},{1,3},{2,0},{3,1},{4,6},{5,7},{6,4},{7,5},{8,10},{9,11},{10,... | collective-permute-start | bytes 393224 | tf_op jit(solution)/shard_map/ppermute | solution.py:237
  38.6 8.8 %collective-permute-start.19 = (bf16[256,256]{1,0:T(8,128)(2,1)S(1)}, bf16[256,256]{1,0:T(8,128)(2,1)S(1)}, u32[]{:S(2)}, u32[]{:S(2)}) collective-permute-start(bf16[256,256]{1,0:T(8,128)(2,1)S(1)} %get-tuple-element.62.refs_3_.refs_4_.refs_0_), channel_id=1, source_target_pairs={{0,6},{1,7},{2,4},{3,5},{4,2},{5,3},{6,0},{7,1},{8,14},{9,15},{10,... | collective-permute-start | bytes 393224 | tf_op jit(solution)/shard_map/ppermute | solution.py:237
  40.7 6.7 %collective-permute-start.18 = (bf16[256,256]{1,0:T(8,128)(2,1)S(1)}, bf16[256,256]{1,0:T(8,128)(2,1)S(1)}, u32[]{:S(2)}, u32[]{:S(2)}) collective-permute-start(bf16[256,256]{1,0:T(8,128)(2,1)S(1)} %get-tuple-element.62.refs_3_.refs_4_.refs_0_), channel_id=1, source_target_pairs={{0,1},{1,0},{2,3},{3,2},{4,5},{5,4},{6,7},{7,6},{8,9},{9,8},{10,11... | collective-permute-start | bytes 393224 | tf_op jit(solution)/shard_map/ppermute | solution.py:237
  42.7 7.5 %collective-permute-start.31 = (bf16[256,256]{1,0:T(8,128)(2,1)S(1)}, bf16[256,256]{1,0:T(8,128)(2,1)S(1)}, u32[]{:S(2)}, u32[]{:S(2)}) collective-permute-start(bf16[256,256]{1,0:T(8,128)(2,1)S(1)} %collective-permute-done.25.refs_11_.refs_12_.refs_8_), channel_id=1, source_target_pairs={{0,6},{1,7},{2,4},{3,5},{4,2},{5,3},{6,0},{7,1},{8,14},{9,15},{10,... | collective-permute-start | bytes 393224 | tf_op jit(solution)/shard_map/ppermute | solution.py:237
  44.3 7.9 %collective-permute-start.29 = (bf16[256,256]{1,0:T(8,128)(2,1)S(1)}, bf16[256,256]{1,0:T(8,128)(2,1)S(1)}, u32[]{:S(2)}, u32[]{:S(2)}) collective-permute-start(bf16[256,256]{1,0:T(8,128)(2,1)S(1)} %collective-permute-done.25.refs_11_.refs_12_.refs_8_), channel_id=1, source_target_pairs={{0,4},{1,5},{2,6},{3,7},{4,0},{5,1},{6,2},{7,3},{8,12},{9,13},{10,... | collective-permute-start | bytes 393224 | tf_op jit(solution)/shard_map/ppermute | solution.py:237
  46.3 6.3 %collective-permute-start.27 = (bf16[256,256]{1,0:T(8,128)(2,1)S(1)}, bf16[256,256]{1,0:T(8,128)(2,1)S(1)}, u32[]{:S(2)}, u32[]{:S(2)}) collective-permute-start(bf16[256,256]{1,0:T(8,128)(2,1)S(1)} %collective-permute-done.25.refs_11_.refs_12_.refs_8_), channel_id=1, source_target_pairs={{0,2},{1,3},{2,0},{3,1},{4,6},{5,7},{6,4},{7,5},{8,10},{9,11},{10,... | collective-permute-start | bytes 393224 | tf_op jit(solution)/shard_map/ppermute | solution.py:237
  47.4 5.4 %collective-permute-start.26 = (bf16[256,256]{1,0:T(8,128)(2,1)S(1)}, bf16[256,256]{1,0:T(8,128)(2,1)S(1)}, u32[]{:S(2)}, u32[]{:S(2)}) collective-permute-start(bf16[256,256]{1,0:T(8,128)(2,1)S(1)} %collective-permute-done.25.refs_11_.refs_12_.refs_8_), channel_id=1, source_target_pairs={{0,1},{1,0},{2,3},{3,2},{4,5},{5,4},{6,7},{7,6},{8,9},{9,8},{10,11... | collective-permute-start | bytes 393224 | tf_op jit(solution)/shard_map/ppermute | solution.py:237
  47.4 5.7 %collective-permute-start.24 = (bf16[256,256]{1,0:T(8,128)(2,1)S(1)}, bf16[256,256]{1,0:T(8,128)(2,1)S(1)}, u32[]{:S(2)}, u32[]{:S(2)}) collective-permute-start(bf16[256,256]{1,0:T(8,128)(2,1)S(1)} %collective-permute-done.23.refs_9_.refs_10_.refs_4_), channel_id=1, source_target_pairs={{0,1},{1,0},{2,3},{3,2},{4,5},{5,4},{6,7},{7,6},{8,9},{9,8},{10,11... | collective-permute-start | bytes 393224 | tf_op jit(solution)/shard_map/ppermute | solution.py:237
  55.7 9.5 %collective-permute-start.33 = (bf16[256,256]{1,0:T(8,128)(2,1)S(1)}, bf16[256,256]{1,0:T(8,128)(2,1)S(1)}, u32[]{:S(2)}, u32[]{:S(2)}) collective-permute-start(bf16[256,256]{1,0:T(8,128)(2,1)S(1)} %shard_map.94), channel_id=1, source_target_pairs={{0,8},{1,9},{2,10},{3,11},{4,12},{5,13},{6,14},{7,15},{8,0},{9,1},... | collective-permute-start | bytes 393224 | tf_op jit(solution)/shard_map/ppermute | solution.py:237
  57.5 7.6 %collective-permute-start.34 = (bf16[256,256]{1,0:T(8,128)(2,1)S(1)}, bf16[256,256]{1,0:T(8,128)(2,1)S(1)}, u32[]{:S(2)}, u32[]{:S(2)}) collective-permute-start(bf16[256,256]{1,0:T(8,128)(2,1)S(1)} %shard_map.95), channel_id=1, source_target_pairs={{0,15},{1,2},{2,1},{3,4},{4,3},{5,6},{6,5},{7,8},{8,7},{9,10},{10,... | collective-permute-start | bytes 393224 | tf_op jit(solution)/shard_map/ppermute | solution.py:241
  (13 other events, 27.9 us)

commit v2 on v1

--- a/solution.py
+++ b/solution.py
@@ -13,6 +13,7 @@
 BF16 = jnp.bfloat16
 F32 = jnp.float32
 STEP = 1 << 32
+HOP = 1 << 28
 
 
 def in_vmem(x):
@@ -134,19 +135,36 @@
     return [m + c for m in (0, *near, *range(count // 2, count, 2)) for c in (0, 1)]
 
 
-def sums_body(count, slots, *refs):
+class Blocks:
+    def __init__(self, places, size):
+        self.count, self.size = len(places), size
+        self.arrays = []
+        index = {}
+        for m in operand_order(self.count):
+            if id(places[m][0]) not in index:
+                index[id(places[m][0])] = len(self.arrays)
+                self.arrays.append(places[m][0])
+        self.places = [(index[id(places[m][0])], places[m][1]) for m in range(self.count)]
+
+    def operands(self):
+        return [in_vmem(x) for x in self.arrays]
+
+    def views(self, refs):
+        return [refs[i].at[pl.ds(first, self.size)] for i, first in self.places]
+
+
+def sums_body(blocks, slots, *refs):
     w_refs, (left_ref, right_ref), refs = refs[:slots], refs[slots : slots + 2], refs[slots + 2 :]
-    order = operand_order(count)
-    blocks = [refs[order.index(m)] for m in range(count)]
-    products(w_refs, left_ref, right_ref, blocks, refs[count:-2], *refs[-2:])
+    used = len(blocks.arrays)
+    products(w_refs, left_ref, right_ref, blocks.views(refs[:used]), refs[used:-2], *refs[-2:])
 
 
 def sums(weights, left_ops, right_ops, blocks, types):
-    count, slots, (terms, size, _) = len(blocks), len(types), right_ops.shape
+    slots, (terms, size, _) = len(types), right_ops.shape
     return pl.pallas_call(
-        functools.partial(sums_body, count, slots),
+        functools.partial(sums_body, blocks, slots),
         out_shape=[pltpu.VMEM((size, size), t) for t in types],
-        in_specs=spec(2 + slots + count),
+        in_specs=spec(2 + slots + len(blocks.arrays)),
         out_specs=spec(slots),
         scratch_shapes=[
             pltpu.VMEM((slots, terms, size, size), BF16),
@@ -154,7 +172,7 @@
         ],
         cost_estimate=cost(1),
         compiler_params=params(12),
-    )(*[in_vmem(x) for x in (*weights, left_ops, right_ops, *[blocks[m] for m in operand_order(count)])])
+    )(*[in_vmem(x) for x in (*weights, left_ops, right_ops)], *blocks.operands())
 
 
 def small(body, shapes, inputs, flops=1):
@@ -168,38 +186,45 @@
     )(*[in_vmem(x) for x in inputs])
 
 
-def keep_body(count, *refs):
-    blocks, stack, squares = refs[:count], refs[count], refs[count + 1]
+def keep_body(blocks, *refs):
+    stack, squares = refs[-2:]
     total = jnp.zeros((8, stack.shape[2]), F32)
-    for m in range(count):
-        value = blocks[m][...]
+    for m, block in enumerate(blocks.views(refs)):
+        value = block[...]
         stack[m] = value
         wide = value.astype(F32)
         total = total + fold_sum(wide * wide)
     squares[...] = jnp.broadcast_to(jnp.sum(total, keepdims=True), squares.shape)
 
 
-def overlap_body(count, me_ref, order_ref, stack, *refs):
-    blocks, overlap = refs[:count], refs[count]
+def overlap_body(blocks, me_ref, order_ref, stack, *refs):
+    overlap = refs[-1]
     me = me_ref[0]
     total = jnp.zeros((8, stack.shape[2]), F32)
-    for m in range(count):
+    for m, block in enumerate(blocks.views(refs)):
         sector = order_ref[jnp.bitwise_xor(me, m)]
         wave = stack[jnp.bitwise_xor(sector, me)].astype(F32)
-        total = total + fold_sum(wave * blocks[m][...].astype(F32))
+        total = total + fold_sum(wave * block[...].astype(F32))
     overlap[...] = jnp.broadcast_to(jnp.sum(total, keepdims=True), overlap.shape)
 
 
 def overlap_with(me, order, stack, blocks):
-    count = len(blocks)
     return pl.pallas_call(
-        functools.partial(overlap_body, count),
+        functools.partial(overlap_body, blocks),
         out_shape=pltpu.VMEM((8, 128), F32),
-        in_specs=[pl.BlockSpec(memory_space=SMEM)] * 2 + spec(1 + count),
+        in_specs=[pl.BlockSpec(memory_space=SMEM)] * 2 + spec(1 + len(blocks.arrays)),
         out_specs=spec(1)[0],
         cost_estimate=cost(1),
         compiler_params=params(8),
-    )(me.reshape(1), order, in_vmem(stack), *[in_vmem(x) for x in blocks])
+    )(me.reshape(1), order, in_vmem(stack), *blocks.operands())
+
+
+def join_body(*refs):
+    *parts, out = refs
+    first = 0
+    for part in parts:
+        out[first : first + part.shape[0]] = part[...]
+        first += part.shape[0]
 
 
 def add_body(total, part, out):
@@ -241,18 +266,39 @@
     return lax.ppermute(x, "op", [(i, (i + (1 if i % 2 else count - 1)) % count) for i in range(count)])
 
 
-def gather_blocks(field, count, prepared=()):
-    blocks = {0: field}
-    half = count // 2
+def touch(x, flops):
+    return pl.pallas_call(
+        lambda given, result: None,
+        out_shape=pltpu.VMEM(x.shape, x.dtype),
+        in_specs=spec(1),
+        out_specs=spec(1)[0],
+        input_output_aliases={0: 0},
+        cost_estimate=cost(flops),
+        compiler_params=params(4),
+    )(in_vmem(x))
+
+
+def gather_blocks(field, count, prepared=(), own=None):
+    got = {0: field}
+    half, size = count // 2, field.shape[0]
     for mask in range(2, half, 2):
-        blocks[mask] = swap(field, count, mask)
-    blocks[half] = swap(field, count, half)
+        got[mask] = swap(field, count, mask)
+    got[half] = touch(swap(field, count, half), HOP)
     for mask in range(2, half, 2):
-        far = after(blocks[half], *prepared) if prepared and mask == 2 else blocks[half]
-        blocks[half + mask] = swap(far, count, mask)
-    for mask in range(0, count, 2):
-        blocks[mask + 1] = swap(blocks[mask], count, 1)
-    return [blocks[m] for m in range(count)]
+        far = after(got[half], *prepared) if prepared and mask == 2 else got[half]
+        got[half + mask] = swap(far, count, mask)
+    got[0] = field if own is None else own
+    places = {m: (x, 0) for m, x in got.items()}
+    early = [m for m in range(2, half, 2) if m.bit_count() == 1]
+    for group in (early, *[[m] for m in range(0, count, 2) if m not in early]):
+        part = got[group[0]]
+        if len(group) > 1:
+            shapes = [pltpu.VMEM((len(group) * size, size), BF16)]
+            (part,) = small(join_body, shapes, [got[m] for m in group])
+        part = swap(part, count, 1)
+        for i, m in enumerate(group):
+            places[m + 1] = (part, i * size)
+    return Blocks(places, size)
 
 
 def after(x, *earlier):
@@ -270,17 +316,16 @@
     def partial_sums(w, blocks):
         (far,) = sums(w[:1], left, right, blocks, (BF16,))
         (other,) = sums((after(w[1], far),), left, right, blocks, (BF16,))
-        near, own = sums((after(w[2], other), w[3]), left, right, blocks, (BF16, F32))
+        near, own = sums((after(w[2], other), w[3]), left, right, blocks, (F32, F32))
         return own, near, (swap(far, count, count // 2), swap_other(other, count), swap(near, count, 1))
 
-    blocks = gather_blocks(field, count, first_w)
-    blocks[0] = psi_block
+    blocks = gather_blocks(field, count, first_w, psi_block)
     own, near, (far_in, other_in, near_in) = partial_sums(first_w, blocks)
-    blocks[0] = after(blocks[0], near)
+    blocks.arrays[0] = after(blocks.arrays[0], near)
     stack, squares = small(
-        functools.partial(keep_body, count),
+        functools.partial(keep_body, blocks),
         [pltpu.VMEM((count, size, size), BF16), pltpu.VMEM((8, 128), F32)],
-        blocks,
+        blocks.arrays,
     )
     total = add(add(after(own, squares), far_in), other_in)
     raw, raw_sent = small(
@@ -291,7 +336,7 @@
     own, near, (far_in, other_in, near_in) = partial_sums(second_w, blocks)
     out_shape = [jax.ShapeDtypeStruct((1, size, size), BF16)]
     (first,) = small(functools.partial(first_body, count), out_shape, (after(raw, near), squares))
-    blocks[0] = after(blocks[0], near)
+    blocks.arrays[0] = after(blocks.arrays[0], near)
     overlap = overlap_with(me, right_order, stack, blocks)
     own, first = lax.optimization_barrier((own, first))
     total = add(add(after(own, overlap), far_in), other_in)

time: 66.1 us -> 65.6 us (level)
    ppermute x34 -> x32, waiting for transfers between devices: 24.1 us -> 23.5 us  [swap(): return lax.ppermute(x, 'op', [(i, i ^ mask) for i in range(count)])]
    pallas_call x8 -> x10, Pallas kernels: 1.87 us -> 1.91 us  [small(): pl.pallas_call(body, out_shape=shapes, in_specs=spec(len(inputs)), out_sp...]
    ppermute x34 -> x32, starting transfers between devices: 23.1 us -> 23.1 us  [swap(): return lax.ppermute(x, 'op', [(i, i ^ mask) for i in range(count)])]
    pallas_call x7 -> x9, Pallas kernels: 9.25 us -> 9.24 us  [the longest x6 8.4 us: sums(): pl.pallas_call(functools.partial(sums_body, blocks, slots), out_shape=[pl...]
  transfers between devices with their start and end apart: 36 -> 34, of which waited for: 19 -> 18; matrix products, arithmetic and copies ran while one was open for 0% -> 0% of each run, Pallas kernels for 15% -> 15%
where the time goes in v2:
time: 65.6 us; the launch traced here: 65.5 us
  starting transfers between devices  28.1 us (43%)
  waiting for transfers between devices  23.7 us (36%)
  Pallas kernels  12.9 us (20%)
  between operations  0.84 us (1%)
    ppermute x32, waiting for transfers between devices, swap(): return lax.ppermute(x, 'op', [(i, i ^ mask) for i in range(count)])  23.5 us
    ppermute x32, starting transfers between devices, swap(): return lax.ppermute(x, 'op', [(i, i ^ mask) for i in range(count)])  23.1 us
    pallas_call x6, Pallas kernels, sums(): pl.pallas_call(functools.partial(sums_body, blocks, slots), out_shape=[pl...  8.4 us
    ppermute x2, starting transfers between devices, swap_other(): lax.ppermute(x, 'op', [(i, (i + (1 if i % 2 else count - 1)) % count) for...  4.95 us
    pallas_call x10, Pallas kernels, small(): pl.pallas_call(body, out_shape=shapes, in_specs=spec(len(inputs)), out_sp...  1.91 us
    pallas_call x1, Pallas kernels, prepare(): pl.pallas_call(functools.partial(prepare_body, count), out_shape=[pltpu.V...  1.71 us
  transfers between devices with their start and end apart: 34, of which 18 were waited for; matrix products, arithmetic and copies ran while one was open for 0% of the time, Pallas kernels for 15%

profile of v2, /device:TPU:0, one launch (start us, length us, event | category | flops | bytes accessed | tf_op | source)
XLA Modules:
  0.0 65.5 jit_solution(4983603312119370459)
XLA Ops:
  0.6 4.1 %collective-permute-start.6 = (bf16[256,256]{1,0:T(8,128)(2,1)}, bf16[256,256]{1,0:T(8,128)(2,1)S(1)}, u32[]{:S(2)}, u32[]{:S(2)}) collective-permute-start(bf16[256,256]{1,0:T(8,128)(2,1)} %bitcast.5), channel_id=1, source_target_pairs={{0,8},{1,9},{2,10},{3,11},{4,12},{5,13},{6,14},{7,15},{8,0},{9,1},... | collective-permute-start | bytes 393224 | tf_op jit(solution)/shard_map/ppermute | solution.py:262
  4.7 1.6 %collective-permute-start.4 = (bf16[256,256]{1,0:T(8,128)(2,1)}, bf16[256,256]{1,0:T(8,128)(2,1)S(1)}, u32[]{:S(2)}, u32[]{:S(2)}) collective-permute-start(bf16[256,256]{1,0:T(8,128)(2,1)} %bitcast.6), channel_id=1, source_target_pairs={{0,4},{1,5},{2,6},{3,7},{4,0},{5,1},{6,2},{7,3},{8,12},{9,13},{10,... | collective-permute-start | bytes 393224 | tf_op jit(solution)/shard_map/ppermute | solution.py:262
  6.3 1.5 %collective-permute-start.3 = (bf16[256,256]{1,0:T(8,128)(2,1)}, bf16[256,256]{1,0:T(8,128)(2,1)S(1)}, u32[]{:S(2)}, u32[]{:S(2)}) collective-permute-start(bf16[256,256]{1,0:T(8,128)(2,1)} %bitcast.7), channel_id=1, source_target_pairs={{0,2},{1,3},{2,0},{3,1},{4,6},{5,7},{6,4},{7,5},{8,10},{9,11},{10,... | collective-permute-start | bytes 393224 | tf_op jit(solution)/shard_map/ppermute | solution.py:262
  8.2 1.7 %shard_map.86 = (bf16[128,256]{1,0:T(8,128)(2,1)S(1)}, bf16[128,256]{1,0:T(8,128)(2,1)S(1)}, bf16[128,256]{1,0:T(8,128)(2,1)S(1)}, bf16[128,256]{1,0:T(8,128)(2,...) custom-call(s32[1]{0:T(128)} %bitcast.me_ref, ...), custom_call_target="tpu_custom_call" | custom-call | flops 1 | bytes 1 | tf_op jit(solution)/shard_map/pallas_call | solution.py:95
  10.0 1.3 %collective-permute-done.6.given = bf16[256,256]{1,0:T(8,128)(2,1)S(1)} collective-permute-done((bf16[256,256]{1,0:T(8,128)(2,1)}, bf16[256,256]{1,0:T(8,128)(2,1)S(1)}, u32[]{:S(2)}, u32[]{:S(2)}) %collective-permute-start.6) | collective-permute-done | bytes 131104 | tf_op jit(solution)/shard_map/ppermute | solution.py:262
  11.4 1.7 %collective-permute-start.12 = (bf16[256,256]{1,0:T(8,128)(2,1)S(1)}, bf16[256,256]{1,0:T(8,128)(2,1)S(1)}, u32[]{:S(2)}, u32[]{:S(2)}) collective-permute-start(bf16[256,256]{1,0:T(8,128)(2,1)S(1)} %shard_map.88.refs_10_.refs_11_.refs_7_), channel_id=1, source_target_pairs={{0,6},{1,7},{2,4},{3,5},{4,2},{5,3},{6,0},{7,1},{8,14},{9,15},{10,... | collective-permute-start | bytes 393224 | tf_op jit(solution)/shard_map/ppermute | solution.py:262
  13.1 1.3 %collective-permute-start.10 = (bf16[256,256]{1,0:T(8,128)(2,1)S(1)}, bf16[256,256]{1,0:T(8,128)(2,1)S(1)}, u32[]{:S(2)}, u32[]{:S(2)}) collective-permute-start(bf16[256,256]{1,0:T(8,128)(2,1)S(1)} %shard_map.88.refs_10_.refs_11_.refs_7_), channel_id=1, source_target_pairs={{0,4},{1,5},{2,6},{3,7},{4,0},{5,1},{6,2},{7,3},{8,12},{9,13},{10,... | collective-permute-start | bytes 393224 | tf_op jit(solution)/shard_map/ppermute | solution.py:262
  14.4 1.8 %collective-permute-done.1.refs_5_.refs_6_.refs_2_ = bf16[256,256]{1,0:T(8,128)(2,1)S(1)} collective-permute-done((bf16[256,256]{1,0:T(8,128)(2,1)}, bf16[256,256]{1,0:T(8,128)(2,1)S(1)}, u32[]{:S(2)}, u32[]{:S(2)}) %collective-permute-start.1) | collective-permute-done | bytes 131104 | tf_op jit(solution)/shard_map/ppermute | solution.py:262
  16.3 2.7 %collective-permute-done.12.refs_16_.refs_17_.refs_13_ = bf16[256,256]{1,0:T(8,128)(2,1)S(1)} collective-permute-done((bf16[256,256]{1,0:T(8,128)(2,1)S(1)}, bf16[256,256]{1,0:T(8,128)(2,1)S(1)}, u32[]{:S(2)}, u32[]{:S(2)}) %collective-permute-start.12) | collective-permute-done | bytes 131104 | tf_op jit(solution)/shard_map/ppermute | solution.py:262
  20.5 1.6 %collective-permute-done.8.refs_12_.refs_13_.refs_9_ = bf16[256,256]{1,0:T(8,128)(2,1)S(1)} collective-permute-done((bf16[256,256]{1,0:T(8,128)(2,1)S(1)}, bf16[256,256]{1,0:T(8,128)(2,1)S(1)}, u32[]{:S(2)}, u32[]{:S(2)}) %collective-permute-start.8) | collective-permute-done | bytes 131104 | tf_op jit(solution)/shard_map/ppermute | solution.py:262
  22.2 1.3 %collective-permute-done.9.refs_13_.refs_14_.refs_10_ = bf16[256,256]{1,0:T(8,128)(2,1)S(1)} collective-permute-done((bf16[256,256]{1,0:T(8,128)(2,1)S(1)}, bf16[256,256]{1,0:T(8,128)(2,1)S(1)}, u32[]{:S(2)}, u32[]{:S(2)}) %collective-permute-start.9) | collective-permute-done | bytes 131104 | tf_op jit(solution)/shard_map/ppermute | solution.py:262
  26.9 2.3 %collective-permute-start.15 = (bf16[256,256]{1,0:T(8,128)(2,1)S(1)}, bf16[256,256]{1,0:T(8,128)(2,1)S(1)}, u32[]{:S(2)}, u32[]{:S(2)}) collective-permute-start(bf16[256,256]{1,0:T(8,128)(2,1)S(1)} %shard_map.90), channel_id=1, source_target_pairs={{0,15},{1,2},{2,1},{3,4},{4,3},{5,6},{6,5},{7,8},{8,7},{9,10},{10,... | collective-permute-start | bytes 393224 | tf_op jit(solution)/shard_map/ppermute | solution.py:266
  29.2 1.8 %shard_map.91 = (f32[256,256]{1,0:T(8,128)S(1)}, f32[256,256]{1,0:T(8,128)S(1)}) custom-call(bf16[128,256]{1,0:T(8,128)(2,1)S(1)} %get-tuple-element.45.refs_0_, bf16[128,256]{1,0:T(8,128)(2,1)S(1)} %get-tuple-element.42.refs_1_, bf16[8,256,256]{2,1,0:T(8,128)(2,1)S(1)} %get-tuple-element.36.refs_1_.refs_2_, ...), custom_call_target="tpu_custom_call" | custom-call | flops 1 | bytes 1 | tf_op jit(solution)/shard_map/pallas_call | solution.py:164
  31.3 2.7 %collective-permute-done.14.part = bf16[256,256]{1,0:T(8,128)(2,1)S(1)} collective-permute-done((bf16[256,256]{1,0:T(8,128)(2,1)S(1)}, bf16[256,256]{1,0:T(8,128)(2,1)S(1)}, u32[]{:S(2)}, u32[]{:S(2)}) %collective-permute-start.14) | collective-permute-done | bytes 131104 | tf_op jit(solution)/shard_map/ppermute | solution.py:262
  34.2 2.6 %collective-permute-start.23 = (bf16[256,256]{1,0:T(8,128)(2,1)S(1)}, bf16[256,256]{1,0:T(8,128)(2,1)S(1)}, u32[]{:S(2)}, u32[]{:S(2)}) collective-permute-start(bf16[256,256]{1,0:T(8,128)(2,1)S(1)} %get-tuple-element.62.refs_3_.refs_4_.refs_0_), channel_id=1, source_target_pairs={{0,8},{1,9},{2,10},{3,11},{4,12},{5,13},{6,14},{7,15},{8,0},{9,1},... | collective-permute-start | bytes 393224 | tf_op jit(solution)/shard_map/ppermute | solution.py:262
  36.9 1.4 %collective-permute-start.21 = (bf16[256,256]{1,0:T(8,128)(2,1)S(1)}, bf16[256,256]{1,0:T(8,128)(2,1)S(1)}, u32[]{:S(2)}, u32[]{:S(2)}) collective-permute-start(bf16[256,256]{1,0:T(8,128)(2,1)S(1)} %get-tuple-element.62.refs_3_.refs_4_.refs_0_), channel_id=1, source_target_pairs={{0,4},{1,5},{2,6},{3,7},{4,0},{5,1},{6,2},{7,3},{8,12},{9,13},{10,... | collective-permute-start | bytes 393224 | tf_op jit(solution)/shard_map/ppermute | solution.py:262
  38.3 2.1 %collective-permute-start.18 = (bf16[256,256]{1,0:T(8,128)(2,1)S(1)}, bf16[256,256]{1,0:T(8,128)(2,1)S(1)}, u32[]{:S(2)}, u32[]{:S(2)}) collective-permute-start(bf16[256,256]{1,0:T(8,128)(2,1)S(1)} %get-tuple-element.62.refs_3_.refs_4_.refs_0_), channel_id=1, source_target_pairs={{0,6},{1,7},{2,4},{3,5},{4,2},{5,3},{6,0},{7,1},{8,14},{9,15},{10,... | collective-permute-start | bytes 393224 | tf_op jit(solution)/shard_map/ppermute | solution.py:262
  40.4 2.4 %collective-permute-done.23.given = bf16[256,256]{1,0:T(8,128)(2,1)S(1)} collective-permute-done((bf16[256,256]{1,0:T(8,128)(2,1)S(1)}, bf16[256,256]{1,0:T(8,128)(2,1)S(1)}, u32[]{:S(2)}, u32[]{:S(2)}) %collective-permute-start.23) | collective-permute-done | bytes 131104 | tf_op jit(solution)/shard_map/ppermute | solution.py:262
  44.2 1.8 %collective-permute-start.27 = (bf16[256,256]{1,0:T(8,128)(2,1)S(1)}, bf16[256,256]{1,0:T(8,128)(2,1)S(1)}, u32[]{:S(2)}, u32[]{:S(2)}) collective-permute-start(bf16[256,256]{1,0:T(8,128)(2,1)S(1)} %shard_map.97.refs_10_.refs_11_.refs_7_), channel_id=1, source_target_pairs={{0,4},{1,5},{2,6},{3,7},{4,0},{5,1},{6,2},{7,3},{8,12},{9,13},{10,... | collective-permute-start | bytes 393224 | tf_op jit(solution)/shard_map/ppermute | solution.py:262
  47.5 2.5 %collective-permute-done.29.refs_16_.refs_17_.refs_13_ = bf16[256,256]{1,0:T(8,128)(2,1)S(1)} collective-permute-done((bf16[256,256]{1,0:T(8,128)(2,1)S(1)}, bf16[256,256]{1,0:T(8,128)(2,1)S(1)}, u32[]{:S(2)}, u32[]{:S(2)}) %collective-permute-start.29) | collective-permute-done | bytes 131104 | tf_op jit(solution)/shard_map/ppermute | solution.py:262
  50.1 1.6 %collective-permute-done.27.refs_14_.refs_15_.refs_11_ = bf16[256,256]{1,0:T(8,128)(2,1)S(1)} collective-permute-done((bf16[256,256]{1,0:T(8,128)(2,1)S(1)}, bf16[256,256]{1,0:T(8,128)(2,1)S(1)}, u32[]{:S(2)}, u32[]{:S(2)}) %collective-permute-start.27) | collective-permute-done | bytes 131104 | tf_op jit(solution)/shard_map/ppermute | solution.py:262
  56.1 1.2 %shard_map.99 = bf16[256,256]{1,0:T(8,128)(2,1)S(1)} custom-call(bf16[128,256]{1,0:T(8,128)(2,1)S(1)} %get-tuple-element.52.refs_0_, bf16[8,256,256]{2,1,0:T(8,128)(2,1)S(1)} %get-tuple-element.36.refs_1_.refs_2_, bf16[8,256,256]{2,1,0:T(8,128)(2,1)S(1)} %get-tuple-element.37.refs_2_.refs_3_, bf16[256,256]{1,0:T(8,128)(2,1)S(1)} %get-tuple-element.62.refs_3_.refs_4_.refs_0_, ...), custom_call_target="tpu_custom_call" | custom-call | flops 1 | bytes 1 | tf_op jit(solution)/shard_map/pallas_call | solution.py:164
  57.3 2.7 %collective-permute-start.32 = (bf16[256,256]{1,0:T(8,128)(2,1)S(1)}, bf16[256,256]{1,0:T(8,128)(2,1)S(1)}, u32[]{:S(2)}, u32[]{:S(2)}) collective-permute-start(bf16[256,256]{1,0:T(8,128)(2,1)S(1)} %shard_map.99), channel_id=1, source_target_pairs={{0,15},{1,2},{2,1},{3,4},{4,3},{5,6},{6,5},{7,8},{8,7},{9,10},{10,... | collective-permute-start | bytes 393224 | tf_op jit(solution)/shard_map/ppermute | solution.py:266
  60.0 1.8 %shard_map.100 = (f32[256,256]{1,0:T(8,128)S(1)}, f32[256,256]{1,0:T(8,128)S(1)}) custom-call(bf16[128,256]{1,0:T(8,128)(2,1)S(1)} %get-tuple-element.53.refs_0_, bf16[128,256]{1,0:T(8,128)(2,1)S(1)} %get-tuple-element.54.refs_1_, bf16[8,256,256]{2,1,0:T(8,128)(2,1)S(1)} %get-tuple-element.36.refs_1_.refs_2_, ...), custom_call_target="tpu_custom_call" | custom-call | flops 1 | bytes 1 | tf_op jit(solution)/shard_map/pallas_call | solution.py:164
  (66 shorter events, 17.0 us)
Async XLA Ops:
  0.6 10.7 %collective-permute-start.6 = (bf16[256,256]{1,0:T(8,128)(2,1)}, bf16[256,256]{1,0:T(8,128)(2,1)S(1)}, u32[]{:S(2)}, u32[]{:S(2)}) collective-permute-start(bf16[256,256]{1,0:T(8,128)(2,1)} %bitcast.5), channel_id=1, source_target_pairs={{0,8},{1,9},{2,10},{3,11},{4,12},{5,13},{6,14},{7,15},{8,0},{9,1},... | collective-permute-start | bytes 393224 | tf_op jit(solution)/shard_map/ppermute | solution.py:262
  4.7 8.3 %collective-permute-start.4 = (bf16[256,256]{1,0:T(8,128)(2,1)}, bf16[256,256]{1,0:T(8,128)(2,1)S(1)}, u32[]{:S(2)}, u32[]{:S(2)}) collective-permute-start(bf16[256,256]{1,0:T(8,128)(2,1)} %bitcast.6), channel_id=1, source_target_pairs={{0,4},{1,5},{2,6},{3,7},{4,0},{5,1},{6,2},{7,3},{8,12},{9,13},{10,... | collective-permute-start | bytes 393224 | tf_op jit(solution)/shard_map/ppermute | solution.py:262
  6.3 8.1 %collective-permute-start.3 = (bf16[256,256]{1,0:T(8,128)(2,1)}, bf16[256,256]{1,0:T(8,128)(2,1)S(1)}, u32[]{:S(2)}, u32[]{:S(2)}) collective-permute-start(bf16[256,256]{1,0:T(8,128)(2,1)} %bitcast.7), channel_id=1, source_target_pairs={{0,2},{1,3},{2,0},{3,1},{4,6},{5,7},{6,4},{7,5},{8,10},{9,11},{10,... | collective-permute-start | bytes 393224 | tf_op jit(solution)/shard_map/ppermute | solution.py:262
  7.8 8.4 %collective-permute-start.1 = (bf16[256,256]{1,0:T(8,128)(2,1)}, bf16[256,256]{1,0:T(8,128)(2,1)S(1)}, u32[]{:S(2)}, u32[]{:S(2)}) collective-permute-start(bf16[256,256]{1,0:T(8,128)(2,1)} %bitcast.8), channel_id=1, source_target_pairs={{0,6},{1,7},{2,4},{3,5},{4,2},{5,3},{6,0},{7,1},{8,14},{9,15},{10,... | collective-permute-start | bytes 393224 | tf_op jit(solution)/shard_map/ppermute | solution.py:262
  9.9 6.3 %collective-permute-start = (bf16[256,256]{1,0:T(8,128)(2,1)S(1)}, bf16[256,256]{1,0:T(8,128)(2,1)S(1)}, u32[]{:S(2)}, u32[]{:S(2)}) collective-permute-start(bf16[256,256]{1,0:T(8,128)(2,1)S(1)} %get-tuple-element.48.refs_3_.refs_4_.refs_0_), channel_id=1, source_target_pairs={{0,1},{1,0},{2,3},{3,2},{4,5},{5,4},{6,7},{7,6},{8,9},{9,8},{10,11... | collective-permute-start | bytes 393224 | tf_op jit(solution)/shard_map/ppermute | solution.py:262
  11.4 7.7 %collective-permute-start.12 = (bf16[256,256]{1,0:T(8,128)(2,1)S(1)}, bf16[256,256]{1,0:T(8,128)(2,1)S(1)}, u32[]{:S(2)}, u32[]{:S(2)}) collective-permute-start(bf16[256,256]{1,0:T(8,128)(2,1)S(1)} %shard_map.88.refs_10_.refs_11_.refs_7_), channel_id=1, source_target_pairs={{0,6},{1,7},{2,4},{3,5},{4,2},{5,3},{6,0},{7,1},{8,14},{9,15},{10,... | collective-permute-start | bytes 393224 | tf_op jit(solution)/shard_map/ppermute | solution.py:262
  13.1 6.9 %collective-permute-start.10 = (bf16[256,256]{1,0:T(8,128)(2,1)S(1)}, bf16[256,256]{1,0:T(8,128)(2,1)S(1)}, u32[]{:S(2)}, u32[]{:S(2)}) collective-permute-start(bf16[256,256]{1,0:T(8,128)(2,1)S(1)} %shard_map.88.refs_10_.refs_11_.refs_7_), channel_id=1, source_target_pairs={{0,4},{1,5},{2,6},{3,7},{4,0},{5,1},{6,2},{7,3},{8,12},{9,13},{10,... | collective-permute-start | bytes 393224 | tf_op jit(solution)/shard_map/ppermute | solution.py:262
  14.4 5.6 %collective-permute-start.7 = (bf16[256,256]{1,0:T(8,128)(2,1)S(1)}, bf16[256,256]{1,0:T(8,128)(2,1)S(1)}, u32[]{:S(2)}, u32[]{:S(2)}) collective-permute-start(bf16[256,256]{1,0:T(8,128)(2,1)S(1)} %shard_map.88.refs_10_.refs_11_.refs_7_), channel_id=1, source_target_pairs={{0,1},{1,0},{2,3},{3,2},{4,5},{5,4},{6,7},{7,6},{8,9},{9,8},{10,11... | collective-permute-start | bytes 393224 | tf_op jit(solution)/shard_map/ppermute | solution.py:262
  16.2 5.9 %collective-permute-start.5 = (bf16[512,256]{1,0:T(8,128)(2,1)S(1)}, bf16[512,256]{1,0:T(8,128)(2,1)S(1)}, u32[]{:S(2)}, u32[]{:S(2)}) collective-permute-start(bf16[512,256]{1,0:T(8,128)(2,1)S(1)} %shard_map.87), channel_id=1, source_target_pairs={{0,1},{1,0},{2,3},{3,2},{4,5},{5,4},{6,7},{7,6},{8,9},{9,8},{10,11... | collective-permute-start | bytes 786440 | tf_op jit(solution)/shard_map/ppermute | solution.py:262
  16.2 5.9 %collective-permute-start.8 = (bf16[256,256]{1,0:T(8,128)(2,1)S(1)}, bf16[256,256]{1,0:T(8,128)(2,1)S(1)}, u32[]{:S(2)}, u32[]{:S(2)}) collective-permute-start(bf16[256,256]{1,0:T(8,128)(2,1)S(1)} %shard_map.88.refs_10_.refs_11_.refs_7_), channel_id=1, source_target_pairs={{0,2},{1,3},{2,0},{3,1},{4,6},{5,7},{6,4},{7,5},{8,10},{9,11},{10,... | collective-permute-start | bytes 393224 | tf_op jit(solution)/shard_map/ppermute | solution.py:262
  24.7 9.3 %collective-permute-start.14 = (bf16[256,256]{1,0:T(8,128)(2,1)S(1)}, bf16[256,256]{1,0:T(8,128)(2,1)S(1)}, u32[]{:S(2)}, u32[]{:S(2)}) collective-permute-start(bf16[256,256]{1,0:T(8,128)(2,1)S(1)} %shard_map.89), channel_id=1, source_target_pairs={{0,8},{1,9},{2,10},{3,11},{4,12},{5,13},{6,14},{7,15},{8,0},{9,1},... | collective-permute-start | bytes 393224 | tf_op jit(solution)/shard_map/ppermute | solution.py:262
  26.9 7.3 %collective-permute-start.15 = (bf16[256,256]{1,0:T(8,128)(2,1)S(1)}, bf16[256,256]{1,0:T(8,128)(2,1)S(1)}, u32[]{:S(2)}, u32[]{:S(2)}) collective-permute-start(bf16[256,256]{1,0:T(8,128)(2,1)S(1)} %shard_map.90), channel_id=1, source_target_pairs={{0,15},{1,2},{2,1},{3,4},{4,3},{5,6},{6,5},{7,8},{8,7},{9,10},{10,... | collective-permute-start | bytes 393224 | tf_op jit(solution)/shard_map/ppermute | solution.py:266
  34.2 8.5 %collective-permute-start.23 = (bf16[256,256]{1,0:T(8,128)(2,1)S(1)}, bf16[256,256]{1,0:T(8,128)(2,1)S(1)}, u32[]{:S(2)}, u32[]{:S(2)}) collective-permute-start(bf16[256,256]{1,0:T(8,128)(2,1)S(1)} %get-tuple-element.62.refs_3_.refs_4_.refs_0_), channel_id=1, source_target_pairs={{0,8},{1,9},{2,10},{3,11},{4,12},{5,13},{6,14},{7,15},{8,0},{9,1},... | collective-permute-start | bytes 393224 | tf_op jit(solution)/shard_map/ppermute | solution.py:262
  36.9 7.3 %collective-permute-start.21 = (bf16[256,256]{1,0:T(8,128)(2,1)S(1)}, bf16[256,256]{1,0:T(8,128)(2,1)S(1)}, u32[]{:S(2)}, u32[]{:S(2)}) collective-permute-start(bf16[256,256]{1,0:T(8,128)(2,1)S(1)} %get-tuple-element.62.refs_3_.refs_4_.refs_0_), channel_id=1, source_target_pairs={{0,4},{1,5},{2,6},{3,7},{4,0},{5,1},{6,2},{7,3},{8,12},{9,13},{10,... | collective-permute-start | bytes 393224 | tf_op jit(solution)/shard_map/ppermute | solution.py:262
  38.3 7.8 %collective-permute-start.20 = (bf16[256,256]{1,0:T(8,128)(2,1)S(1)}, bf16[256,256]{1,0:T(8,128)(2,1)S(1)}, u32[]{:S(2)}, u32[]{:S(2)}) collective-permute-start(bf16[256,256]{1,0:T(8,128)(2,1)S(1)} %get-tuple-element.62.refs_3_.refs_4_.refs_0_), channel_id=1, source_target_pairs={{0,2},{1,3},{2,0},{3,1},{4,6},{5,7},{6,4},{7,5},{8,10},{9,11},{10,... | collective-permute-start | bytes 393224 | tf_op jit(solution)/shard_map/ppermute | solution.py:262
  38.3 8.7 %collective-permute-start.18 = (bf16[256,256]{1,0:T(8,128)(2,1)S(1)}, bf16[256,256]{1,0:T(8,128)(2,1)S(1)}, u32[]{:S(2)}, u32[]{:S(2)}) collective-permute-start(bf16[256,256]{1,0:T(8,128)(2,1)S(1)} %get-tuple-element.62.refs_3_.refs_4_.refs_0_), channel_id=1, source_target_pairs={{0,6},{1,7},{2,4},{3,5},{4,2},{5,3},{6,0},{7,1},{8,14},{9,15},{10,... | collective-permute-start | bytes 393224 | tf_op jit(solution)/shard_map/ppermute | solution.py:262
  40.3 6.7 %collective-permute-start.17 = (bf16[256,256]{1,0:T(8,128)(2,1)S(1)}, bf16[256,256]{1,0:T(8,128)(2,1)S(1)}, u32[]{:S(2)}, u32[]{:S(2)}) collective-permute-start(bf16[256,256]{1,0:T(8,128)(2,1)S(1)} %get-tuple-element.62.refs_3_.refs_4_.refs_0_), channel_id=1, source_target_pairs={{0,1},{1,0},{2,3},{3,2},{4,5},{5,4},{6,7},{7,6},{8,9},{9,8},{10,11... | collective-permute-start | bytes 393224 | tf_op jit(solution)/shard_map/ppermute | solution.py:262
  42.7 7.3 %collective-permute-start.29 = (bf16[256,256]{1,0:T(8,128)(2,1)S(1)}, bf16[256,256]{1,0:T(8,128)(2,1)S(1)}, u32[]{:S(2)}, u32[]{:S(2)}) collective-permute-start(bf16[256,256]{1,0:T(8,128)(2,1)S(1)} %shard_map.97.refs_10_.refs_11_.refs_7_), channel_id=1, source_target_pairs={{0,6},{1,7},{2,4},{3,5},{4,2},{5,3},{6,0},{7,1},{8,14},{9,15},{10,... | collective-permute-start | bytes 393224 | tf_op jit(solution)/shard_map/ppermute | solution.py:262
  44.2 7.4 %collective-permute-start.27 = (bf16[256,256]{1,0:T(8,128)(2,1)S(1)}, bf16[256,256]{1,0:T(8,128)(2,1)S(1)}, u32[]{:S(2)}, u32[]{:S(2)}) collective-permute-start(bf16[256,256]{1,0:T(8,128)(2,1)S(1)} %shard_map.97.refs_10_.refs_11_.refs_7_), channel_id=1, source_target_pairs={{0,4},{1,5},{2,6},{3,7},{4,0},{5,1},{6,2},{7,3},{8,12},{9,13},{10,... | collective-permute-start | bytes 393224 | tf_op jit(solution)/shard_map/ppermute | solution.py:262
  46.0 6.2 %collective-permute-start.25 = (bf16[256,256]{1,0:T(8,128)(2,1)S(1)}, bf16[256,256]{1,0:T(8,128)(2,1)S(1)}, u32[]{:S(2)}, u32[]{:S(2)}) collective-permute-start(bf16[256,256]{1,0:T(8,128)(2,1)S(1)} %shard_map.97.refs_10_.refs_11_.refs_7_), channel_id=1, source_target_pairs={{0,2},{1,3},{2,0},{3,1},{4,6},{5,7},{6,4},{7,5},{8,10},{9,11},{10,... | collective-permute-start | bytes 393224 | tf_op jit(solution)/shard_map/ppermute | solution.py:262
  47.0 5.3 %collective-permute-start.24 = (bf16[256,256]{1,0:T(8,128)(2,1)S(1)}, bf16[256,256]{1,0:T(8,128)(2,1)S(1)}, u32[]{:S(2)}, u32[]{:S(2)}) collective-permute-start(bf16[256,256]{1,0:T(8,128)(2,1)S(1)} %shard_map.97.refs_10_.refs_11_.refs_7_), channel_id=1, source_target_pairs={{0,1},{1,0},{2,3},{3,2},{4,5},{5,4},{6,7},{7,6},{8,9},{9,8},{10,11... | collective-permute-start | bytes 393224 | tf_op jit(solution)/shard_map/ppermute | solution.py:262
  47.0 6.8 %collective-permute-start.22 = (bf16[512,256]{1,0:T(8,128)(2,1)S(1)}, bf16[512,256]{1,0:T(8,128)(2,1)S(1)}, u32[]{:S(2)}, u32[]{:S(2)}) collective-permute-start(bf16[512,256]{1,0:T(8,128)(2,1)S(1)} %shard_map.96), channel_id=1, source_target_pairs={{0,1},{1,0},{2,3},{3,2},{4,5},{5,4},{6,7},{7,6},{8,9},{9,8},{10,11... | collective-permute-start | bytes 786440 | tf_op jit(solution)/shard_map/ppermute | solution.py:262
  55.0 9.6 %collective-permute-start.31 = (bf16[256,256]{1,0:T(8,128)(2,1)S(1)}, bf16[256,256]{1,0:T(8,128)(2,1)S(1)}, u32[]{:S(2)}, u32[]{:S(2)}) collective-permute-start(bf16[256,256]{1,0:T(8,128)(2,1)S(1)} %shard_map.98), channel_id=1, source_target_pairs={{0,8},{1,9},{2,10},{3,11},{4,12},{5,13},{6,14},{7,15},{8,0},{9,1},... | collective-permute-start | bytes 393224 | tf_op jit(solution)/shard_map/ppermute | solution.py:262
  57.3 7.3 %collective-permute-start.32 = (bf16[256,256]{1,0:T(8,128)(2,1)S(1)}, bf16[256,256]{1,0:T(8,128)(2,1)S(1)}, u32[]{:S(2)}, u32[]{:S(2)}) collective-permute-start(bf16[256,256]{1,0:T(8,128)(2,1)S(1)} %shard_map.99), channel_id=1, source_target_pairs={{0,15},{1,2},{2,1},{3,4},{4,3},{5,6},{6,5},{7,8},{8,7},{9,10},{10,... | collective-permute-start | bytes 393224 | tf_op jit(solution)/shard_map/ppermute | solution.py:266
  (11 other events, 24.4 us)

commit v3 on v2

--- a/solution.py
+++ b/solution.py
@@ -125,9 +125,10 @@
         for t in range(slots):
             inner[t, k * size : (k + 1) * size, :] = value[t * size : (t + 1) * size]
     for t in range(slots):
-        row = jnp.concatenate([left_ref[k] for k in range(terms)], axis=1)
-        total = jnp.dot(row, inner[t], preferred_element_type=F32)
-        outs[t][...] = total.astype(outs[t].dtype)
+        for rows in (slice(0, size // 2), slice(size // 2, size)):
+            row = jnp.concatenate([left_ref[k, rows, :] for k in range(terms)], axis=1)
+            total = jnp.dot(row, inner[t], preferred_element_type=F32)
+            outs[t][rows, :] = total.astype(outs[t].dtype)
 
 
 def operand_order(count):

time: 65.6 us -> 65.3 us (level)
  Pallas kernels: 12.9 us -> 12.2 us
  transfers between devices with their start and end apart: 34 -> 34, of which waited for: 18 -> 17; matrix products, arithmetic and copies ran while one was open for 0% -> 0% of each run, Pallas kernels for 15% -> 14%
where the time goes in v3:
time: 65.3 us; the launch traced here: 65.1 us
  starting transfers between devices  28.1 us (43%)
  waiting for transfers between devices  24 us (37%)
  Pallas kernels  12.2 us (19%)
  between operations  0.84 us (1%)
    ppermute x32, waiting for transfers between devices, swap(): return lax.ppermute(x, 'op', [(i, i ^ mask) for i in range(count)])  24 us
    ppermute x32, starting transfers between devices, swap(): return lax.ppermute(x, 'op', [(i, i ^ mask) for i in range(count)])  23.1 us
    pallas_call x6, Pallas kernels, sums(): pl.pallas_call(functools.partial(sums_body, blocks, slots), out_shape=[pl...  7.77 us
    ppermute x2, starting transfers between devices, swap_other(): lax.ppermute(x, 'op', [(i, (i + (1 if i % 2 else count - 1)) % count) for...  4.93 us
    pallas_call x10, Pallas kernels, small(): pl.pallas_call(body, out_shape=shapes, in_specs=spec(len(inputs)), out_sp...  1.91 us
    pallas_call x1, Pallas kernels, prepare(): pl.pallas_call(functools.partial(prepare_body, count), out_shape=[pltpu.V...  1.71 us
  transfers between devices with their start and end apart: 34, of which 17 were waited for; matrix products, arithmetic and copies ran while one was open for 0% of the time, Pallas kernels for 14%

profile of v3, /device:TPU:0, one launch (start us, length us, event | category | flops | bytes accessed | tf_op | source)
XLA Modules:
  0.0 65.1 jit_solution(9343643218491411504)
XLA Ops:
  0.6 4.1 %collective-permute-start.6 = (bf16[256,256]{1,0:T(8,128)(2,1)}, bf16[256,256]{1,0:T(8,128)(2,1)S(1)}, u32[]{:S(2)}, u32[]{:S(2)}) collective-permute-start(bf16[256,256]{1,0:T(8,128)(2,1)} %bitcast.5), channel_id=1, source_target_pairs={{0,8},{1,9},{2,10},{3,11},{4,12},{5,13},{6,14},{7,15},{8,0},{9,1},... | collective-permute-start | bytes 393224 | tf_op jit(solution)/shard_map/ppermute | solution.py:263
  4.7 1.6 %collective-permute-start.4 = (bf16[256,256]{1,0:T(8,128)(2,1)}, bf16[256,256]{1,0:T(8,128)(2,1)S(1)}, u32[]{:S(2)}, u32[]{:S(2)}) collective-permute-start(bf16[256,256]{1,0:T(8,128)(2,1)} %bitcast.6), channel_id=1, source_target_pairs={{0,4},{1,5},{2,6},{3,7},{4,0},{5,1},{6,2},{7,3},{8,12},{9,13},{10,... | collective-permute-start | bytes 393224 | tf_op jit(solution)/shard_map/ppermute | solution.py:263
  6.3 1.5 %collective-permute-start.3 = (bf16[256,256]{1,0:T(8,128)(2,1)}, bf16[256,256]{1,0:T(8,128)(2,1)S(1)}, u32[]{:S(2)}, u32[]{:S(2)}) collective-permute-start(bf16[256,256]{1,0:T(8,128)(2,1)} %bitcast.7), channel_id=1, source_target_pairs={{0,2},{1,3},{2,0},{3,1},{4,6},{5,7},{6,4},{7,5},{8,10},{9,11},{10,... | collective-permute-start | bytes 393224 | tf_op jit(solution)/shard_map/ppermute | solution.py:263
  8.2 1.7 %shard_map.86 = (bf16[128,256]{1,0:T(8,128)(2,1)S(1)}, bf16[128,256]{1,0:T(8,128)(2,1)S(1)}, bf16[128,256]{1,0:T(8,128)(2,1)S(1)}, bf16[128,256]{1,0:T(8,128)(2,...) custom-call(s32[1]{0:T(128)} %bitcast.me_ref, ...), custom_call_target="tpu_custom_call" | custom-call | flops 1 | bytes 1 | tf_op jit(solution)/shard_map/pallas_call | solution.py:95
  10.0 1.3 %collective-permute-done.6.given = bf16[256,256]{1,0:T(8,128)(2,1)S(1)} collective-permute-done((bf16[256,256]{1,0:T(8,128)(2,1)}, bf16[256,256]{1,0:T(8,128)(2,1)S(1)}, u32[]{:S(2)}, u32[]{:S(2)}) %collective-permute-start.6) | collective-permute-done | bytes 131104 | tf_op jit(solution)/shard_map/ppermute | solution.py:263
  11.4 1.7 %collective-permute-start.12 = (bf16[256,256]{1,0:T(8,128)(2,1)S(1)}, bf16[256,256]{1,0:T(8,128)(2,1)S(1)}, u32[]{:S(2)}, u32[]{:S(2)}) collective-permute-start(bf16[256,256]{1,0:T(8,128)(2,1)S(1)} %shard_map.88.refs_10_.refs_11_.refs_7_), channel_id=1, source_target_pairs={{0,6},{1,7},{2,4},{3,5},{4,2},{5,3},{6,0},{7,1},{8,14},{9,15},{10,... | collective-permute-start | bytes 393224 | tf_op jit(solution)/shard_map/ppermute | solution.py:263
  13.1 1.3 %collective-permute-start.10 = (bf16[256,256]{1,0:T(8,128)(2,1)S(1)}, bf16[256,256]{1,0:T(8,128)(2,1)S(1)}, u32[]{:S(2)}, u32[]{:S(2)}) collective-permute-start(bf16[256,256]{1,0:T(8,128)(2,1)S(1)} %shard_map.88.refs_10_.refs_11_.refs_7_), channel_id=1, source_target_pairs={{0,4},{1,5},{2,6},{3,7},{4,0},{5,1},{6,2},{7,3},{8,12},{9,13},{10,... | collective-permute-start | bytes 393224 | tf_op jit(solution)/shard_map/ppermute | solution.py:263
  14.4 1.8 %collective-permute-done.1.refs_5_.refs_6_.refs_2_ = bf16[256,256]{1,0:T(8,128)(2,1)S(1)} collective-permute-done((bf16[256,256]{1,0:T(8,128)(2,1)}, bf16[256,256]{1,0:T(8,128)(2,1)S(1)}, u32[]{:S(2)}, u32[]{:S(2)}) %collective-permute-start.1) | collective-permute-done | bytes 131104 | tf_op jit(solution)/shard_map/ppermute | solution.py:263
  16.3 2.7 %collective-permute-done.12.refs_16_.refs_17_.refs_13_ = bf16[256,256]{1,0:T(8,128)(2,1)S(1)} collective-permute-done((bf16[256,256]{1,0:T(8,128)(2,1)S(1)}, bf16[256,256]{1,0:T(8,128)(2,1)S(1)}, u32[]{:S(2)}, u32[]{:S(2)}) %collective-permute-start.12) | collective-permute-done | bytes 131104 | tf_op jit(solution)/shard_map/ppermute | solution.py:263
  20.5 1.6 %collective-permute-done.8.refs_12_.refs_13_.refs_9_ = bf16[256,256]{1,0:T(8,128)(2,1)S(1)} collective-permute-done((bf16[256,256]{1,0:T(8,128)(2,1)S(1)}, bf16[256,256]{1,0:T(8,128)(2,1)S(1)}, u32[]{:S(2)}, u32[]{:S(2)}) %collective-permute-start.8) | collective-permute-done | bytes 131104 | tf_op jit(solution)/shard_map/ppermute | solution.py:263
  22.2 1.3 %collective-permute-done.9.refs_13_.refs_14_.refs_10_ = bf16[256,256]{1,0:T(8,128)(2,1)S(1)} collective-permute-done((bf16[256,256]{1,0:T(8,128)(2,1)S(1)}, bf16[256,256]{1,0:T(8,128)(2,1)S(1)}, u32[]{:S(2)}, u32[]{:S(2)}) %collective-permute-start.9) | collective-permute-done | bytes 131104 | tf_op jit(solution)/shard_map/ppermute | solution.py:263
  26.6 2.3 %collective-permute-start.15 = (bf16[256,256]{1,0:T(8,128)(2,1)S(1)}, bf16[256,256]{1,0:T(8,128)(2,1)S(1)}, u32[]{:S(2)}, u32[]{:S(2)}) collective-permute-start(bf16[256,256]{1,0:T(8,128)(2,1)S(1)} %shard_map.90), channel_id=1, source_target_pairs={{0,15},{1,2},{2,1},{3,4},{4,3},{5,6},{6,5},{7,8},{8,7},{9,10},{10,... | collective-permute-start | bytes 393224 | tf_op jit(solution)/shard_map/ppermute | solution.py:267
  28.9 1.8 %shard_map.91 = (f32[256,256]{1,0:T(8,128)S(1)}, f32[256,256]{1,0:T(8,128)S(1)}) custom-call(bf16[128,256]{1,0:T(8,128)(2,1)S(1)} %get-tuple-element.45.refs_0_, bf16[128,256]{1,0:T(8,128)(2,1)S(1)} %get-tuple-element.42.refs_1_, bf16[8,256,256]{2,1,0:T(8,128)(2,1)S(1)} %get-tuple-element.36.refs_1_.refs_2_, ...), custom_call_target="tpu_custom_call" | custom-call | flops 1 | bytes 1 | tf_op jit(solution)/shard_map/pallas_call | solution.py:165
  31.0 2.8 %collective-permute-done.14.part = bf16[256,256]{1,0:T(8,128)(2,1)S(1)} collective-permute-done((bf16[256,256]{1,0:T(8,128)(2,1)S(1)}, bf16[256,256]{1,0:T(8,128)(2,1)S(1)}, u32[]{:S(2)}, u32[]{:S(2)}) %collective-permute-start.14) | collective-permute-done | bytes 131104 | tf_op jit(solution)/shard_map/ppermute | solution.py:263
  34.0 2.7 %collective-permute-start.23 = (bf16[256,256]{1,0:T(8,128)(2,1)S(1)}, bf16[256,256]{1,0:T(8,128)(2,1)S(1)}, u32[]{:S(2)}, u32[]{:S(2)}) collective-permute-start(bf16[256,256]{1,0:T(8,128)(2,1)S(1)} %get-tuple-element.62.refs_3_.refs_4_.refs_0_), channel_id=1, source_target_pairs={{0,8},{1,9},{2,10},{3,11},{4,12},{5,13},{6,14},{7,15},{8,0},{9,1},... | collective-permute-start | bytes 393224 | tf_op jit(solution)/shard_map/ppermute | solution.py:263
  36.7 1.4 %collective-permute-start.21 = (bf16[256,256]{1,0:T(8,128)(2,1)S(1)}, bf16[256,256]{1,0:T(8,128)(2,1)S(1)}, u32[]{:S(2)}, u32[]{:S(2)}) collective-permute-start(bf16[256,256]{1,0:T(8,128)(2,1)S(1)} %get-tuple-element.62.refs_3_.refs_4_.refs_0_), channel_id=1, source_target_pairs={{0,4},{1,5},{2,6},{3,7},{4,0},{5,1},{6,2},{7,3},{8,12},{9,13},{10,... | collective-permute-start | bytes 393224 | tf_op jit(solution)/shard_map/ppermute | solution.py:263
  38.1 2.1 %collective-permute-start.18 = (bf16[256,256]{1,0:T(8,128)(2,1)S(1)}, bf16[256,256]{1,0:T(8,128)(2,1)S(1)}, u32[]{:S(2)}, u32[]{:S(2)}) collective-permute-start(bf16[256,256]{1,0:T(8,128)(2,1)S(1)} %get-tuple-element.62.refs_3_.refs_4_.refs_0_), channel_id=1, source_target_pairs={{0,6},{1,7},{2,4},{3,5},{4,2},{5,3},{6,0},{7,1},{8,14},{9,15},{10,... | collective-permute-start | bytes 393224 | tf_op jit(solution)/shard_map/ppermute | solution.py:263
  40.2 2.4 %collective-permute-done.23.given = bf16[256,256]{1,0:T(8,128)(2,1)S(1)} collective-permute-done((bf16[256,256]{1,0:T(8,128)(2,1)S(1)}, bf16[256,256]{1,0:T(8,128)(2,1)S(1)}, u32[]{:S(2)}, u32[]{:S(2)}) %collective-permute-start.23) | collective-permute-done | bytes 131104 | tf_op jit(solution)/shard_map/ppermute | solution.py:263
  44.1 1.8 %collective-permute-start.27 = (bf16[256,256]{1,0:T(8,128)(2,1)S(1)}, bf16[256,256]{1,0:T(8,128)(2,1)S(1)}, u32[]{:S(2)}, u32[]{:S(2)}) collective-permute-start(bf16[256,256]{1,0:T(8,128)(2,1)S(1)} %shard_map.97.refs_10_.refs_11_.refs_7_), channel_id=1, source_target_pairs={{0,4},{1,5},{2,6},{3,7},{4,0},{5,1},{6,2},{7,3},{8,12},{9,13},{10,... | collective-permute-start | bytes 393224 | tf_op jit(solution)/shard_map/ppermute | solution.py:263
  47.4 2.5 %collective-permute-done.29.refs_16_.refs_17_.refs_13_ = bf16[256,256]{1,0:T(8,128)(2,1)S(1)} collective-permute-done((bf16[256,256]{1,0:T(8,128)(2,1)S(1)}, bf16[256,256]{1,0:T(8,128)(2,1)S(1)}, u32[]{:S(2)}, u32[]{:S(2)}) %collective-permute-start.29) | collective-permute-done | bytes 131104 | tf_op jit(solution)/shard_map/ppermute | solution.py:263
  49.9 1.6 %collective-permute-done.27.refs_14_.refs_15_.refs_11_ = bf16[256,256]{1,0:T(8,128)(2,1)S(1)} collective-permute-done((bf16[256,256]{1,0:T(8,128)(2,1)S(1)}, bf16[256,256]{1,0:T(8,128)(2,1)S(1)}, u32[]{:S(2)}, u32[]{:S(2)}) %collective-permute-start.27) | collective-permute-done | bytes 131104 | tf_op jit(solution)/shard_map/ppermute | solution.py:263
  56.9 2.6 %collective-permute-start.32 = (bf16[256,256]{1,0:T(8,128)(2,1)S(1)}, bf16[256,256]{1,0:T(8,128)(2,1)S(1)}, u32[]{:S(2)}, u32[]{:S(2)}) collective-permute-start(bf16[256,256]{1,0:T(8,128)(2,1)S(1)} %shard_map.99), channel_id=1, source_target_pairs={{0,15},{1,2},{2,1},{3,4},{4,3},{5,6},{6,5},{7,8},{8,7},{9,10},{10,... | collective-permute-start | bytes 393224 | tf_op jit(solution)/shard_map/ppermute | solution.py:267
  59.5 1.8 %shard_map.100 = (f32[256,256]{1,0:T(8,128)S(1)}, f32[256,256]{1,0:T(8,128)S(1)}) custom-call(bf16[128,256]{1,0:T(8,128)(2,1)S(1)} %get-tuple-element.53.refs_0_, bf16[128,256]{1,0:T(8,128)(2,1)S(1)} %get-tuple-element.54.refs_1_, bf16[8,256,256]{2,1,0:T(8,128)(2,1)S(1)} %get-tuple-element.36.refs_1_.refs_2_, ...), custom_call_target="tpu_custom_call" | custom-call | flops 1 | bytes 1 | tf_op jit(solution)/shard_map/pallas_call | solution.py:165
  63.0 1.3 %collective-permute-done.31.part = bf16[256,256]{1,0:T(8,128)(2,1)S(1)} collective-permute-done((bf16[256,256]{1,0:T(8,128)(2,1)S(1)}, bf16[256,256]{1,0:T(8,128)(2,1)S(1)}, u32[]{:S(2)}, u32[]{:S(2)}) %collective-permute-start.31) | collective-permute-done | bytes 131104 | tf_op jit(solution)/shard_map/ppermute | solution.py:263
  (66 shorter events, 16.4 us)
Async XLA Ops:
  0.6 10.7 %collective-permute-start.6 = (bf16[256,256]{1,0:T(8,128)(2,1)}, bf16[256,256]{1,0:T(8,128)(2,1)S(1)}, u32[]{:S(2)}, u32[]{:S(2)}) collective-permute-start(bf16[256,256]{1,0:T(8,128)(2,1)} %bitcast.5), channel_id=1, source_target_pairs={{0,8},{1,9},{2,10},{3,11},{4,12},{5,13},{6,14},{7,15},{8,0},{9,1},... | collective-permute-start | bytes 393224 | tf_op jit(solution)/shard_map/ppermute | solution.py:263
  4.7 8.3 %collective-permute-start.4 = (bf16[256,256]{1,0:T(8,128)(2,1)}, bf16[256,256]{1,0:T(8,128)(2,1)S(1)}, u32[]{:S(2)}, u32[]{:S(2)}) collective-permute-start(bf16[256,256]{1,0:T(8,128)(2,1)} %bitcast.6), channel_id=1, source_target_pairs={{0,4},{1,5},{2,6},{3,7},{4,0},{5,1},{6,2},{7,3},{8,12},{9,13},{10,... | collective-permute-start | bytes 393224 | tf_op jit(solution)/shard_map/ppermute | solution.py:263
  6.3 8.1 %collective-permute-start.3 = (bf16[256,256]{1,0:T(8,128)(2,1)}, bf16[256,256]{1,0:T(8,128)(2,1)S(1)}, u32[]{:S(2)}, u32[]{:S(2)}) collective-permute-start(bf16[256,256]{1,0:T(8,128)(2,1)} %bitcast.7), channel_id=1, source_target_pairs={{0,2},{1,3},{2,0},{3,1},{4,6},{5,7},{6,4},{7,5},{8,10},{9,11},{10,... | collective-permute-start | bytes 393224 | tf_op jit(solution)/shard_map/ppermute | solution.py:263
  7.8 8.4 %collective-permute-start.1 = (bf16[256,256]{1,0:T(8,128)(2,1)}, bf16[256,256]{1,0:T(8,128)(2,1)S(1)}, u32[]{:S(2)}, u32[]{:S(2)}) collective-permute-start(bf16[256,256]{1,0:T(8,128)(2,1)} %bitcast.8), channel_id=1, source_target_pairs={{0,6},{1,7},{2,4},{3,5},{4,2},{5,3},{6,0},{7,1},{8,14},{9,15},{10,... | collective-permute-start | bytes 393224 | tf_op jit(solution)/shard_map/ppermute | solution.py:263
  9.9 6.3 %collective-permute-start = (bf16[256,256]{1,0:T(8,128)(2,1)S(1)}, bf16[256,256]{1,0:T(8,128)(2,1)S(1)}, u32[]{:S(2)}, u32[]{:S(2)}) collective-permute-start(bf16[256,256]{1,0:T(8,128)(2,1)S(1)} %get-tuple-element.48.refs_3_.refs_4_.refs_0_), channel_id=1, source_target_pairs={{0,1},{1,0},{2,3},{3,2},{4,5},{5,4},{6,7},{7,6},{8,9},{9,8},{10,11... | collective-permute-start | bytes 393224 | tf_op jit(solution)/shard_map/ppermute | solution.py:263
  11.4 7.7 %collective-permute-start.12 = (bf16[256,256]{1,0:T(8,128)(2,1)S(1)}, bf16[256,256]{1,0:T(8,128)(2,1)S(1)}, u32[]{:S(2)}, u32[]{:S(2)}) collective-permute-start(bf16[256,256]{1,0:T(8,128)(2,1)S(1)} %shard_map.88.refs_10_.refs_11_.refs_7_), channel_id=1, source_target_pairs={{0,6},{1,7},{2,4},{3,5},{4,2},{5,3},{6,0},{7,1},{8,14},{9,15},{10,... | collective-permute-start | bytes 393224 | tf_op jit(solution)/shard_map/ppermute | solution.py:263
  13.1 6.9 %collective-permute-start.10 = (bf16[256,256]{1,0:T(8,128)(2,1)S(1)}, bf16[256,256]{1,0:T(8,128)(2,1)S(1)}, u32[]{:S(2)}, u32[]{:S(2)}) collective-permute-start(bf16[256,256]{1,0:T(8,128)(2,1)S(1)} %shard_map.88.refs_10_.refs_11_.refs_7_), channel_id=1, source_target_pairs={{0,4},{1,5},{2,6},{3,7},{4,0},{5,1},{6,2},{7,3},{8,12},{9,13},{10,... | collective-permute-start | bytes 393224 | tf_op jit(solution)/shard_map/ppermute | solution.py:263
  14.4 5.6 %collective-permute-start.7 = (bf16[256,256]{1,0:T(8,128)(2,1)S(1)}, bf16[256,256]{1,0:T(8,128)(2,1)S(1)}, u32[]{:S(2)}, u32[]{:S(2)}) collective-permute-start(bf16[256,256]{1,0:T(8,128)(2,1)S(1)} %shard_map.88.refs_10_.refs_11_.refs_7_), channel_id=1, source_target_pairs={{0,1},{1,0},{2,3},{3,2},{4,5},{5,4},{6,7},{7,6},{8,9},{9,8},{10,11... | collective-permute-start | bytes 393224 | tf_op jit(solution)/shard_map/ppermute | solution.py:263
  16.2 5.9 %collective-permute-start.5 = (bf16[512,256]{1,0:T(8,128)(2,1)S(1)}, bf16[512,256]{1,0:T(8,128)(2,1)S(1)}, u32[]{:S(2)}, u32[]{:S(2)}) collective-permute-start(bf16[512,256]{1,0:T(8,128)(2,1)S(1)} %shard_map.87), channel_id=1, source_target_pairs={{0,1},{1,0},{2,3},{3,2},{4,5},{5,4},{6,7},{7,6},{8,9},{9,8},{10,11... | collective-permute-start | bytes 786440 | tf_op jit(solution)/shard_map/ppermute | solution.py:263
  16.2 5.9 %collective-permute-start.8 = (bf16[256,256]{1,0:T(8,128)(2,1)S(1)}, bf16[256,256]{1,0:T(8,128)(2,1)S(1)}, u32[]{:S(2)}, u32[]{:S(2)}) collective-permute-start(bf16[256,256]{1,0:T(8,128)(2,1)S(1)} %shard_map.88.refs_10_.refs_11_.refs_7_), channel_id=1, source_target_pairs={{0,2},{1,3},{2,0},{3,1},{4,6},{5,7},{6,4},{7,5},{8,10},{9,11},{10,... | collective-permute-start | bytes 393224 | tf_op jit(solution)/shard_map/ppermute | solution.py:263
  24.5 9.3 %collective-permute-start.14 = (bf16[256,256]{1,0:T(8,128)(2,1)S(1)}, bf16[256,256]{1,0:T(8,128)(2,1)S(1)}, u32[]{:S(2)}, u32[]{:S(2)}) collective-permute-start(bf16[256,256]{1,0:T(8,128)(2,1)S(1)} %shard_map.89), channel_id=1, source_target_pairs={{0,8},{1,9},{2,10},{3,11},{4,12},{5,13},{6,14},{7,15},{8,0},{9,1},... | collective-permute-start | bytes 393224 | tf_op jit(solution)/shard_map/ppermute | solution.py:263
  26.6 7.3 %collective-permute-start.15 = (bf16[256,256]{1,0:T(8,128)(2,1)S(1)}, bf16[256,256]{1,0:T(8,128)(2,1)S(1)}, u32[]{:S(2)}, u32[]{:S(2)}) collective-permute-start(bf16[256,256]{1,0:T(8,128)(2,1)S(1)} %shard_map.90), channel_id=1, source_target_pairs={{0,15},{1,2},{2,1},{3,4},{4,3},{5,6},{6,5},{7,8},{8,7},{9,10},{10,... | collective-permute-start | bytes 393224 | tf_op jit(solution)/shard_map/ppermute | solution.py:267
  34.0 8.6 %collective-permute-start.23 = (bf16[256,256]{1,0:T(8,128)(2,1)S(1)}, bf16[256,256]{1,0:T(8,128)(2,1)S(1)}, u32[]{:S(2)}, u32[]{:S(2)}) collective-permute-start(bf16[256,256]{1,0:T(8,128)(2,1)S(1)} %get-tuple-element.62.refs_3_.refs_4_.refs_0_), channel_id=1, source_target_pairs={{0,8},{1,9},{2,10},{3,11},{4,12},{5,13},{6,14},{7,15},{8,0},{9,1},... | collective-permute-start | bytes 393224 | tf_op jit(solution)/shard_map/ppermute | solution.py:263
  36.7 7.3 %collective-permute-start.21 = (bf16[256,256]{1,0:T(8,128)(2,1)S(1)}, bf16[256,256]{1,0:T(8,128)(2,1)S(1)}, u32[]{:S(2)}, u32[]{:S(2)}) collective-permute-start(bf16[256,256]{1,0:T(8,128)(2,1)S(1)} %get-tuple-element.62.refs_3_.refs_4_.refs_0_), channel_id=1, source_target_pairs={{0,4},{1,5},{2,6},{3,7},{4,0},{5,1},{6,2},{7,3},{8,12},{9,13},{10,... | collective-permute-start | bytes 393224 | tf_op jit(solution)/shard_map/ppermute | solution.py:263
  38.1 7.8 %collective-permute-start.20 = (bf16[256,256]{1,0:T(8,128)(2,1)S(1)}, bf16[256,256]{1,0:T(8,128)(2,1)S(1)}, u32[]{:S(2)}, u32[]{:S(2)}) collective-permute-start(bf16[256,256]{1,0:T(8,128)(2,1)S(1)} %get-tuple-element.62.refs_3_.refs_4_.refs_0_), channel_id=1, source_target_pairs={{0,2},{1,3},{2,0},{3,1},{4,6},{5,7},{6,4},{7,5},{8,10},{9,11},{10,... | collective-permute-start | bytes 393224 | tf_op jit(solution)/shard_map/ppermute | solution.py:263
  38.1 8.7 %collective-permute-start.18 = (bf16[256,256]{1,0:T(8,128)(2,1)S(1)}, bf16[256,256]{1,0:T(8,128)(2,1)S(1)}, u32[]{:S(2)}, u32[]{:S(2)}) collective-permute-start(bf16[256,256]{1,0:T(8,128)(2,1)S(1)} %get-tuple-element.62.refs_3_.refs_4_.refs_0_), channel_id=1, source_target_pairs={{0,6},{1,7},{2,4},{3,5},{4,2},{5,3},{6,0},{7,1},{8,14},{9,15},{10,... | collective-permute-start | bytes 393224 | tf_op jit(solution)/shard_map/ppermute | solution.py:263
  40.2 6.7 %collective-permute-start.17 = (bf16[256,256]{1,0:T(8,128)(2,1)S(1)}, bf16[256,256]{1,0:T(8,128)(2,1)S(1)}, u32[]{:S(2)}, u32[]{:S(2)}) collective-permute-start(bf16[256,256]{1,0:T(8,128)(2,1)S(1)} %get-tuple-element.62.refs_3_.refs_4_.refs_0_), channel_id=1, source_target_pairs={{0,1},{1,0},{2,3},{3,2},{4,5},{5,4},{6,7},{7,6},{8,9},{9,8},{10,11... | collective-permute-start | bytes 393224 | tf_op jit(solution)/shard_map/ppermute | solution.py:263
  42.6 7.3 %collective-permute-start.29 = (bf16[256,256]{1,0:T(8,128)(2,1)S(1)}, bf16[256,256]{1,0:T(8,128)(2,1)S(1)}, u32[]{:S(2)}, u32[]{:S(2)}) collective-permute-start(bf16[256,256]{1,0:T(8,128)(2,1)S(1)} %shard_map.97.refs_10_.refs_11_.refs_7_), channel_id=1, source_target_pairs={{0,6},{1,7},{2,4},{3,5},{4,2},{5,3},{6,0},{7,1},{8,14},{9,15},{10,... | collective-permute-start | bytes 393224 | tf_op jit(solution)/shard_map/ppermute | solution.py:263
  44.1 7.4 %collective-permute-start.27 = (bf16[256,256]{1,0:T(8,128)(2,1)S(1)}, bf16[256,256]{1,0:T(8,128)(2,1)S(1)}, u32[]{:S(2)}, u32[]{:S(2)}) collective-permute-start(bf16[256,256]{1,0:T(8,128)(2,1)S(1)} %shard_map.97.refs_10_.refs_11_.refs_7_), channel_id=1, source_target_pairs={{0,4},{1,5},{2,6},{3,7},{4,0},{5,1},{6,2},{7,3},{8,12},{9,13},{10,... | collective-permute-start | bytes 393224 | tf_op jit(solution)/shard_map/ppermute | solution.py:263
  45.9 6.2 %collective-permute-start.25 = (bf16[256,256]{1,0:T(8,128)(2,1)S(1)}, bf16[256,256]{1,0:T(8,128)(2,1)S(1)}, u32[]{:S(2)}, u32[]{:S(2)}) collective-permute-start(bf16[256,256]{1,0:T(8,128)(2,1)S(1)} %shard_map.97.refs_10_.refs_11_.refs_7_), channel_id=1, source_target_pairs={{0,2},{1,3},{2,0},{3,1},{4,6},{5,7},{6,4},{7,5},{8,10},{9,11},{10,... | collective-permute-start | bytes 393224 | tf_op jit(solution)/shard_map/ppermute | solution.py:263
  46.9 5.3 %collective-permute-start.24 = (bf16[256,256]{1,0:T(8,128)(2,1)S(1)}, bf16[256,256]{1,0:T(8,128)(2,1)S(1)}, u32[]{:S(2)}, u32[]{:S(2)}) collective-permute-start(bf16[256,256]{1,0:T(8,128)(2,1)S(1)} %shard_map.97.refs_10_.refs_11_.refs_7_), channel_id=1, source_target_pairs={{0,1},{1,0},{2,3},{3,2},{4,5},{5,4},{6,7},{7,6},{8,9},{9,8},{10,11... | collective-permute-start | bytes 393224 | tf_op jit(solution)/shard_map/ppermute | solution.py:263
  46.9 6.8 %collective-permute-start.22 = (bf16[512,256]{1,0:T(8,128)(2,1)S(1)}, bf16[512,256]{1,0:T(8,128)(2,1)S(1)}, u32[]{:S(2)}, u32[]{:S(2)}) collective-permute-start(bf16[512,256]{1,0:T(8,128)(2,1)S(1)} %shard_map.96), channel_id=1, source_target_pairs={{0,1},{1,0},{2,3},{3,2},{4,5},{5,4},{6,7},{7,6},{8,9},{9,8},{10,11... | collective-permute-start | bytes 786440 | tf_op jit(solution)/shard_map/ppermute | solution.py:263
  54.7 9.6 %collective-permute-start.31 = (bf16[256,256]{1,0:T(8,128)(2,1)S(1)}, bf16[256,256]{1,0:T(8,128)(2,1)S(1)}, u32[]{:S(2)}, u32[]{:S(2)}) collective-permute-start(bf16[256,256]{1,0:T(8,128)(2,1)S(1)} %shard_map.98), channel_id=1, source_target_pairs={{0,8},{1,9},{2,10},{3,11},{4,12},{5,13},{6,14},{7,15},{8,0},{9,1},... | collective-permute-start | bytes 393224 | tf_op jit(solution)/shard_map/ppermute | solution.py:263
  56.9 7.5 %collective-permute-start.32 = (bf16[256,256]{1,0:T(8,128)(2,1)S(1)}, bf16[256,256]{1,0:T(8,128)(2,1)S(1)}, u32[]{:S(2)}, u32[]{:S(2)}) collective-permute-start(bf16[256,256]{1,0:T(8,128)(2,1)S(1)} %shard_map.99), channel_id=1, source_target_pairs={{0,15},{1,2},{2,1},{3,4},{4,3},{5,6},{6,5},{7,8},{8,7},{9,10},{10,... | collective-permute-start | bytes 393224 | tf_op jit(solution)/shard_map/ppermute | solution.py:267
  (11 other events, 24.7 us)

commit v4 on v3

--- a/solution.py
+++ b/solution.py
@@ -286,13 +286,15 @@
         got[mask] = swap(field, count, mask)
     got[half] = touch(swap(field, count, half), HOP)
     for mask in range(2, half, 2):
-        far = after(got[half], *prepared) if prepared and mask == 2 else got[half]
-        got[half + mask] = swap(far, count, mask)
+        got[half + mask] = swap(got[half], count, mask)
     got[0] = field if own is None else own
     places = {m: (x, 0) for m, x in got.items()}
-    early = [m for m in range(2, half, 2) if m.bit_count() == 1]
-    for group in (early, *[[m] for m in range(0, count, 2) if m not in early]):
+    near = range(2, half, 2)
+    early, late = ([m for m in near if (m.bit_count() == 1) == single] for single in (True, False))
+    for group in (early, [0], [half, *late], *[[half + m] for m in near]):
         part = got[group[0]]
+        if prepared and group == [0]:
+            part = after(part, *prepared)
         if len(group) > 1:
             shapes = [pltpu.VMEM((len(group) * size, size), BF16)]
             (part,) = small(join_body, shapes, [got[m] for m in group])

time: 65.3 us -> 64.8 us (level)
  waiting for transfers between devices: 24 us -> 21.9 us
  starting transfers between devices: 28.1 us -> 29.6 us
    ppermute x32 -> x30, waiting for transfers between devices: 24 us -> 21.2 us  [swap(): return lax.ppermute(x, 'op', [(i, i ^ mask) for i in range(count)])]
    ppermute x32 -> x30, starting transfers between devices: 23.1 us -> 25.1 us  [swap(): return lax.ppermute(x, 'op', [(i, i ^ mask) for i in range(count)])]
    ppermute x2, waiting for transfers between devices: 0.01 us -> 0.77 us  [swap_other(): lax.ppermute(x, 'op', [(i, (i + (1 if i % 2 else count - 1)) % count) for...]
    pallas_call x10 -> x12, Pallas kernels: 1.91 us -> 1.94 us  [small(): pl.pallas_call(body, out_shape=shapes, in_specs=spec(len(inputs)), out_sp...]
  transfers between devices with their start and end apart: 34 -> 32, of which waited for: 17 -> 18; matrix products, arithmetic and copies ran while one was open for 0% -> 0% of each run, Pallas kernels for 14% -> 15%
where the time goes in v4:
time: 64.8 us; the launch traced here: 64.6 us
  starting transfers between devices  29.6 us (46%)
  waiting for transfers between devices  21.9 us (34%)
  Pallas kernels  12.3 us (19%)
  between operations  0.83 us (1%)
    ppermute x30, starting transfers between devices, swap(): return lax.ppermute(x, 'op', [(i, i ^ mask) for i in range(count)])  25.1 us
    ppermute x30, waiting for transfers between devices, swap(): return lax.ppermute(x, 'op', [(i, i ^ mask) for i in range(count)])  21.2 us
    pallas_call x6, Pallas kernels, sums(): pl.pallas_call(functools.partial(sums_body, blocks, slots), out_shape=[pl...  7.77 us
    ppermute x2, starting transfers between devices, swap_other(): lax.ppermute(x, 'op', [(i, (i + (1 if i % 2 else count - 1)) % count) for...  4.51 us
    pallas_call x12, Pallas kernels, small(): pl.pallas_call(body, out_shape=shapes, in_specs=spec(len(inputs)), out_sp...  1.94 us
    pallas_call x1, Pallas kernels, prepare(): pl.pallas_call(functools.partial(prepare_body, count), out_shape=[pltpu.V...  1.71 us
  transfers between devices with their start and end apart: 32, of which 18 were waited for; matrix products, arithmetic and copies ran while one was open for 0% of the time, Pallas kernels for 15%

profile of v4, /device:TPU:0, one launch (start us, length us, event | category | flops | bytes accessed | tf_op | source)
XLA Modules:
  0.0 64.6 jit_solution(10289897009310940165)
XLA Ops:
  0.6 4.1 %collective-permute-start.2 = (bf16[256,256]{1,0:T(8,128)(2,1)}, bf16[256,256]{1,0:T(8,128)(2,1)S(1)}, u32[]{:S(2)}, u32[]{:S(2)}) collective-permute-start(bf16[256,256]{1,0:T(8,128)(2,1)} %bitcast.5), channel_id=1, source_target_pairs={{0,8},{1,9},{2,10},{3,11},{4,12},{5,13},{6,14},{7,15},{8,0},{9,1},... | collective-permute-start | bytes 393224 | tf_op jit(solution)/shard_map/ppermute | solution.py:263
  4.7 1.6 %collective-permute-start.5 = (bf16[256,256]{1,0:T(8,128)(2,1)}, bf16[256,256]{1,0:T(8,128)(2,1)S(1)}, u32[]{:S(2)}, u32[]{:S(2)}) collective-permute-start(bf16[256,256]{1,0:T(8,128)(2,1)} %bitcast.6), channel_id=1, source_target_pairs={{0,4},{1,5},{2,6},{3,7},{4,0},{5,1},{6,2},{7,3},{8,12},{9,13},{10,... | collective-permute-start | bytes 393224 | tf_op jit(solution)/shard_map/ppermute | solution.py:263
  6.3 1.5 %collective-permute-start.4 = (bf16[256,256]{1,0:T(8,128)(2,1)}, bf16[256,256]{1,0:T(8,128)(2,1)S(1)}, u32[]{:S(2)}, u32[]{:S(2)}) collective-permute-start(bf16[256,256]{1,0:T(8,128)(2,1)} %bitcast.7), channel_id=1, source_target_pairs={{0,2},{1,3},{2,0},{3,1},{4,6},{5,7},{6,4},{7,5},{8,10},{9,11},{10,... | collective-permute-start | bytes 393224 | tf_op jit(solution)/shard_map/ppermute | solution.py:263
  8.2 1.7 %shard_map.86 = (bf16[128,256]{1,0:T(8,128)(2,1)S(1)}, bf16[128,256]{1,0:T(8,128)(2,1)S(1)}, bf16[128,256]{1,0:T(8,128)(2,1)S(1)}, bf16[128,256]{1,0:T(8,128)(2,...) custom-call(s32[1]{0:T(128)} %bitcast.me_ref, ...), custom_call_target="tpu_custom_call" | custom-call | flops 1 | bytes 1 | tf_op jit(solution)/shard_map/pallas_call | solution.py:95
  10.0 1.3 %collective-permute-done.2.given = bf16[256,256]{1,0:T(8,128)(2,1)S(1)} collective-permute-done((bf16[256,256]{1,0:T(8,128)(2,1)}, bf16[256,256]{1,0:T(8,128)(2,1)S(1)}, u32[]{:S(2)}, u32[]{:S(2)}) %collective-permute-start.2) | collective-permute-done | bytes 131104 | tf_op jit(solution)/shard_map/ppermute | solution.py:263
  11.4 1.7 %collective-permute-start.11 = (bf16[256,256]{1,0:T(8,128)(2,1)S(1)}, bf16[256,256]{1,0:T(8,128)(2,1)S(1)}, u32[]{:S(2)}, u32[]{:S(2)}) collective-permute-start(bf16[256,256]{1,0:T(8,128)(2,1)S(1)} %shard_map.87.refs_0_.refs_10_.refs_11_.refs_7_), channel_id=1, source_target_pairs={{0,6},{1,7},{2,4},{3,5},{4,2},{5,3},{6,0},{7,1},{8,14},{9,15},{10,... | collective-permute-start | bytes 393224 | tf_op jit(solution)/shard_map/ppermute | solution.py:263
  13.1 1.3 %collective-permute-start.9 = (bf16[256,256]{1,0:T(8,128)(2,1)S(1)}, bf16[256,256]{1,0:T(8,128)(2,1)S(1)}, u32[]{:S(2)}, u32[]{:S(2)}) collective-permute-start(bf16[256,256]{1,0:T(8,128)(2,1)S(1)} %shard_map.87.refs_0_.refs_10_.refs_11_.refs_7_), channel_id=1, source_target_pairs={{0,4},{1,5},{2,6},{3,7},{4,0},{5,1},{6,2},{7,3},{8,12},{9,13},{10,... | collective-permute-start | bytes 393224 | tf_op jit(solution)/shard_map/ppermute | solution.py:263
  14.4 1.3 %collective-permute-start.7 = (bf16[256,256]{1,0:T(8,128)(2,1)S(1)}, bf16[256,256]{1,0:T(8,128)(2,1)S(1)}, u32[]{:S(2)}, u32[]{:S(2)}) collective-permute-start(bf16[256,256]{1,0:T(8,128)(2,1)S(1)} %shard_map.87.refs_0_.refs_10_.refs_11_.refs_7_), channel_id=1, source_target_pairs={{0,2},{1,3},{2,0},{3,1},{4,6},{5,7},{6,4},{7,5},{8,10},{9,11},{10,... | collective-permute-start | bytes 393224 | tf_op jit(solution)/shard_map/ppermute | solution.py:263
  16.9 2.2 %collective-permute-done.11.refs_15_.refs_16_.refs_12_ = bf16[256,256]{1,0:T(8,128)(2,1)S(1)} collective-permute-done((bf16[256,256]{1,0:T(8,128)(2,1)S(1)}, bf16[256,256]{1,0:T(8,128)(2,1)S(1)}, u32[]{:S(2)}, u32[]{:S(2)}) %collective-permute-start.11) | collective-permute-done | bytes 131104 | tf_op jit(solution)/shard_map/ppermute | solution.py:263
  23.4 1.9 %collective-permute-start.13 = (bf16[256,256]{1,0:T(8,128)(2,1)S(1)}, bf16[256,256]{1,0:T(8,128)(2,1)S(1)}, u32[]{:S(2)}, u32[]{:S(2)}) collective-permute-start(bf16[256,256]{1,0:T(8,128)(2,1)S(1)} %shard_map.90), channel_id=1, source_target_pairs={{0,8},{1,9},{2,10},{3,11},{4,12},{5,13},{6,14},{7,15},{8,0},{9,1},... | collective-permute-start | bytes 393224 | tf_op jit(solution)/shard_map/ppermute | solution.py:263
  26.4 1.9 %collective-permute-start.14 = (bf16[256,256]{1,0:T(8,128)(2,1)S(1)}, bf16[256,256]{1,0:T(8,128)(2,1)S(1)}, u32[]{:S(2)}, u32[]{:S(2)}) collective-permute-start(bf16[256,256]{1,0:T(8,128)(2,1)S(1)} %shard_map.91), channel_id=1, source_target_pairs={{0,15},{1,2},{2,1},{3,4},{4,3},{5,6},{6,5},{7,8},{8,7},{9,10},{10,... | collective-permute-start | bytes 393224 | tf_op jit(solution)/shard_map/ppermute | solution.py:267
  28.3 1.8 %shard_map.92 = (f32[256,256]{1,0:T(8,128)S(1)}, f32[256,256]{1,0:T(8,128)S(1)}) custom-call(bf16[128,256]{1,0:T(8,128)(2,1)S(1)} %get-tuple-element.45.refs_0_, bf16[128,256]{1,0:T(8,128)(2,1)S(1)} %get-tuple-element.42.refs_1_, bf16[8,256,256]{2,1,0:T(8,128)(2,1)S(1)} %get-tuple-element.36.refs_1_.refs_2_, ...), custom_call_target="tpu_custom_call" | custom-call | flops 1 | bytes 1 | tf_op jit(solution)/shard_map/pallas_call | solution.py:165
  30.4 2.4 %collective-permute-done.13.part = bf16[256,256]{1,0:T(8,128)(2,1)S(1)} collective-permute-done((bf16[256,256]{1,0:T(8,128)(2,1)S(1)}, bf16[256,256]{1,0:T(8,128)(2,1)S(1)}, u32[]{:S(2)}, u32[]{:S(2)}) %collective-permute-start.13) | collective-permute-done | bytes 131104 | tf_op jit(solution)/shard_map/ppermute | solution.py:263
  33.7 2.8 %collective-permute-start.18 = (bf16[256,256]{1,0:T(8,128)(2,1)S(1)}, bf16[256,256]{1,0:T(8,128)(2,1)S(1)}, u32[]{:S(2)}, u32[]{:S(2)}) collective-permute-start(bf16[256,256]{1,0:T(8,128)(2,1)S(1)} %get-tuple-element.62.refs_3_.refs_4_.refs_0_), channel_id=1, source_target_pairs={{0,8},{1,9},{2,10},{3,11},{4,12},{5,13},{6,14},{7,15},{8,0},{9,1},... | collective-permute-start | bytes 393224 | tf_op jit(solution)/shard_map/ppermute | solution.py:263
  37.6 2.4 %collective-permute-start.17 = (bf16[256,256]{1,0:T(8,128)(2,1)S(1)}, bf16[256,256]{1,0:T(8,128)(2,1)S(1)}, u32[]{:S(2)}, u32[]{:S(2)}) collective-permute-start(bf16[256,256]{1,0:T(8,128)(2,1)S(1)} %get-tuple-element.62.refs_3_.refs_4_.refs_0_), channel_id=1, source_target_pairs={{0,6},{1,7},{2,4},{3,5},{4,2},{5,3},{6,0},{7,1},{8,14},{9,15},{10,... | collective-permute-start | bytes 393224 | tf_op jit(solution)/shard_map/ppermute | solution.py:263
  40.0 2.2 %collective-permute-done.18.given = bf16[256,256]{1,0:T(8,128)(2,1)S(1)} collective-permute-done((bf16[256,256]{1,0:T(8,128)(2,1)S(1)}, bf16[256,256]{1,0:T(8,128)(2,1)S(1)}, u32[]{:S(2)}, u32[]{:S(2)}) %collective-permute-start.18) | collective-permute-done | bytes 131104 | tf_op jit(solution)/shard_map/ppermute | solution.py:263
  42.3 1.4 %collective-permute-done.21.refs_1_.refs_9_.refs_10_.refs_6_ = bf16[256,256]{1,0:T(8,128)(2,1)S(1)} collective-permute-done((bf16[256,256]{1,0:T(8,128)(2,1)S(1)}, bf16[256,256]{1,0:T(8,128)(2,1)S(1)}, u32[]{:S(2)}, u32[]{:S(2)}) %collective-permute-start.21) | collective-permute-done | bytes 131104 | tf_op jit(solution)/shard_map/ppermute | solution.py:263
  43.7 2.0 %collective-permute-start.25 = (bf16[256,256]{1,0:T(8,128)(2,1)S(1)}, bf16[256,256]{1,0:T(8,128)(2,1)S(1)}, u32[]{:S(2)}, u32[]{:S(2)}) collective-permute-start(bf16[256,256]{1,0:T(8,128)(2,1)S(1)} %shard_map.97.refs_0_.refs_10_.refs_11_.refs_7_), channel_id=1, source_target_pairs={{0,4},{1,5},{2,6},{3,7},{4,0},{5,1},{6,2},{7,3},{8,12},{9,13},{10,... | collective-permute-start | bytes 393224 | tf_op jit(solution)/shard_map/ppermute | solution.py:263
  46.8 2.8 %collective-permute-done.27.refs_15_.refs_16_.refs_12_ = bf16[256,256]{1,0:T(8,128)(2,1)S(1)} collective-permute-done((bf16[256,256]{1,0:T(8,128)(2,1)S(1)}, bf16[256,256]{1,0:T(8,128)(2,1)S(1)}, u32[]{:S(2)}, u32[]{:S(2)}) %collective-permute-start.27) | collective-permute-done | bytes 131104 | tf_op jit(solution)/shard_map/ppermute | solution.py:263
  49.6 2.0 %collective-permute-done.25.refs_13_.refs_14_.refs_10_ = bf16[256,256]{1,0:T(8,128)(2,1)S(1)} collective-permute-done((bf16[256,256]{1,0:T(8,128)(2,1)S(1)}, bf16[256,256]{1,0:T(8,128)(2,1)S(1)}, u32[]{:S(2)}, u32[]{:S(2)}) %collective-permute-start.25) | collective-permute-done | bytes 131104 | tf_op jit(solution)/shard_map/ppermute | solution.py:263
  54.2 1.1 %collective-permute-start.29 = (bf16[256,256]{1,0:T(8,128)(2,1)S(1)}, bf16[256,256]{1,0:T(8,128)(2,1)S(1)}, u32[]{:S(2)}, u32[]{:S(2)}) collective-permute-start(bf16[256,256]{1,0:T(8,128)(2,1)S(1)} %shard_map.100), channel_id=1, source_target_pairs={{0,8},{1,9},{2,10},{3,11},{4,12},{5,13},{6,14},{7,15},{8,0},{9,1},... | collective-permute-start | bytes 393224 | tf_op jit(solution)/shard_map/ppermute | solution.py:263
  56.3 2.6 %collective-permute-start.30 = (bf16[256,256]{1,0:T(8,128)(2,1)S(1)}, bf16[256,256]{1,0:T(8,128)(2,1)S(1)}, u32[]{:S(2)}, u32[]{:S(2)}) collective-permute-start(bf16[256,256]{1,0:T(8,128)(2,1)S(1)} %shard_map.101), channel_id=1, source_target_pairs={{0,15},{1,2},{2,1},{3,4},{4,3},{5,6},{6,5},{7,8},{8,7},{9,10},{10,... | collective-permute-start | bytes 393224 | tf_op jit(solution)/shard_map/ppermute | solution.py:267
  58.9 1.8 %shard_map.102 = (f32[256,256]{1,0:T(8,128)S(1)}, f32[256,256]{1,0:T(8,128)S(1)}) custom-call(bf16[128,256]{1,0:T(8,128)(2,1)S(1)} %get-tuple-element.53.refs_0_, bf16[128,256]{1,0:T(8,128)(2,1)S(1)} %get-tuple-element.54.refs_1_, bf16[8,256,256]{2,1,0:T(8,128)(2,1)S(1)} %get-tuple-element.36.refs_1_.refs_2_, ...), custom_call_target="tpu_custom_call" | custom-call | flops 1 | bytes 1 | tf_op jit(solution)/shard_map/pallas_call | solution.py:165
  62.4 1.4 %collective-permute-done.29.part = bf16[256,256]{1,0:T(8,128)(2,1)S(1)} collective-permute-done((bf16[256,256]{1,0:T(8,128)(2,1)S(1)}, bf16[256,256]{1,0:T(8,128)(2,1)S(1)}, u32[]{:S(2)}, u32[]{:S(2)}) %collective-permute-start.29) | collective-permute-done | bytes 131104 | tf_op jit(solution)/shard_map/ppermute | solution.py:263
  (64 shorter events, 16.5 us)
Async XLA Ops:
  0.6 10.7 %collective-permute-start.2 = (bf16[256,256]{1,0:T(8,128)(2,1)}, bf16[256,256]{1,0:T(8,128)(2,1)S(1)}, u32[]{:S(2)}, u32[]{:S(2)}) collective-permute-start(bf16[256,256]{1,0:T(8,128)(2,1)} %bitcast.5), channel_id=1, source_target_pairs={{0,8},{1,9},{2,10},{3,11},{4,12},{5,13},{6,14},{7,15},{8,0},{9,1},... | collective-permute-start | bytes 393224 | tf_op jit(solution)/shard_map/ppermute | solution.py:263
  4.7 8.3 %collective-permute-start.5 = (bf16[256,256]{1,0:T(8,128)(2,1)}, bf16[256,256]{1,0:T(8,128)(2,1)S(1)}, u32[]{:S(2)}, u32[]{:S(2)}) collective-permute-start(bf16[256,256]{1,0:T(8,128)(2,1)} %bitcast.6), channel_id=1, source_target_pairs={{0,4},{1,5},{2,6},{3,7},{4,0},{5,1},{6,2},{7,3},{8,12},{9,13},{10,... | collective-permute-start | bytes 393224 | tf_op jit(solution)/shard_map/ppermute | solution.py:263
  6.3 8.1 %collective-permute-start.4 = (bf16[256,256]{1,0:T(8,128)(2,1)}, bf16[256,256]{1,0:T(8,128)(2,1)S(1)}, u32[]{:S(2)}, u32[]{:S(2)}) collective-permute-start(bf16[256,256]{1,0:T(8,128)(2,1)} %bitcast.7), channel_id=1, source_target_pairs={{0,2},{1,3},{2,0},{3,1},{4,6},{5,7},{6,4},{7,5},{8,10},{9,11},{10,... | collective-permute-start | bytes 393224 | tf_op jit(solution)/shard_map/ppermute | solution.py:263
  7.8 8.5 %collective-permute-start.1 = (bf16[256,256]{1,0:T(8,128)(2,1)}, bf16[256,256]{1,0:T(8,128)(2,1)S(1)}, u32[]{:S(2)}, u32[]{:S(2)}) collective-permute-start(bf16[256,256]{1,0:T(8,128)(2,1)} %bitcast.8), channel_id=1, source_target_pairs={{0,6},{1,7},{2,4},{3,5},{4,2},{5,3},{6,0},{7,1},{8,14},{9,15},{10,... | collective-permute-start | bytes 393224 | tf_op jit(solution)/shard_map/ppermute | solution.py:263
  9.9 6.4 %collective-permute-start = (bf16[256,256]{1,0:T(8,128)(2,1)S(1)}, bf16[256,256]{1,0:T(8,128)(2,1)S(1)}, u32[]{:S(2)}, u32[]{:S(2)}) collective-permute-start(bf16[256,256]{1,0:T(8,128)(2,1)S(1)} %get-tuple-element.48.refs_3_.refs_4_.refs_0_), channel_id=1, source_target_pairs={{0,1},{1,0},{2,3},{3,2},{4,5},{5,4},{6,7},{7,6},{8,9},{9,8},{10,11... | collective-permute-start | bytes 393224 | tf_op jit(solution)/shard_map/ppermute | solution.py:263
  11.4 7.7 %collective-permute-start.11 = (bf16[256,256]{1,0:T(8,128)(2,1)S(1)}, bf16[256,256]{1,0:T(8,128)(2,1)S(1)}, u32[]{:S(2)}, u32[]{:S(2)}) collective-permute-start(bf16[256,256]{1,0:T(8,128)(2,1)S(1)} %shard_map.87.refs_0_.refs_10_.refs_11_.refs_7_), channel_id=1, source_target_pairs={{0,6},{1,7},{2,4},{3,5},{4,2},{5,3},{6,0},{7,1},{8,14},{9,15},{10,... | collective-permute-start | bytes 393224 | tf_op jit(solution)/shard_map/ppermute | solution.py:263
  13.1 6.9 %collective-permute-start.9 = (bf16[256,256]{1,0:T(8,128)(2,1)S(1)}, bf16[256,256]{1,0:T(8,128)(2,1)S(1)}, u32[]{:S(2)}, u32[]{:S(2)}) collective-permute-start(bf16[256,256]{1,0:T(8,128)(2,1)S(1)} %shard_map.87.refs_0_.refs_10_.refs_11_.refs_7_), channel_id=1, source_target_pairs={{0,4},{1,5},{2,6},{3,7},{4,0},{5,1},{6,2},{7,3},{8,12},{9,13},{10,... | collective-permute-start | bytes 393224 | tf_op jit(solution)/shard_map/ppermute | solution.py:263
  14.4 6.6 %collective-permute-start.7 = (bf16[256,256]{1,0:T(8,128)(2,1)S(1)}, bf16[256,256]{1,0:T(8,128)(2,1)S(1)}, u32[]{:S(2)}, u32[]{:S(2)}) collective-permute-start(bf16[256,256]{1,0:T(8,128)(2,1)S(1)} %shard_map.87.refs_0_.refs_10_.refs_11_.refs_7_), channel_id=1, source_target_pairs={{0,2},{1,3},{2,0},{3,1},{4,6},{5,7},{6,4},{7,5},{8,10},{9,11},{10,... | collective-permute-start | bytes 393224 | tf_op jit(solution)/shard_map/ppermute | solution.py:263
  16.3 6.1 %collective-permute-start.6 = (bf16[512,256]{1,0:T(8,128)(2,1)S(1)}, bf16[512,256]{1,0:T(8,128)(2,1)S(1)}, u32[]{:S(2)}, u32[]{:S(2)}) collective-permute-start(bf16[512,256]{1,0:T(8,128)(2,1)S(1)} %shard_map.89), channel_id=1, source_target_pairs={{0,1},{1,0},{2,3},{3,2},{4,5},{5,4},{6,7},{7,6},{8,9},{9,8},{10,11... | collective-permute-start | bytes 786440 | tf_op jit(solution)/shard_map/ppermute | solution.py:263
  16.3 6.0 %collective-permute-start.3 = (bf16[512,256]{1,0:T(8,128)(2,1)S(1)}, bf16[512,256]{1,0:T(8,128)(2,1)S(1)}, u32[]{:S(2)}, u32[]{:S(2)}) collective-permute-start(bf16[512,256]{1,0:T(8,128)(2,1)S(1)} %shard_map.88), channel_id=1, source_target_pairs={{0,1},{1,0},{2,3},{3,2},{4,5},{5,4},{6,7},{7,6},{8,9},{9,8},{10,11... | collective-permute-start | bytes 786440 | tf_op jit(solution)/shard_map/ppermute | solution.py:263
  23.4 9.4 %collective-permute-start.13 = (bf16[256,256]{1,0:T(8,128)(2,1)S(1)}, bf16[256,256]{1,0:T(8,128)(2,1)S(1)}, u32[]{:S(2)}, u32[]{:S(2)}) collective-permute-start(bf16[256,256]{1,0:T(8,128)(2,1)S(1)} %shard_map.90), channel_id=1, source_target_pairs={{0,8},{1,9},{2,10},{3,11},{4,12},{5,13},{6,14},{7,15},{8,0},{9,1},... | collective-permute-start | bytes 393224 | tf_op jit(solution)/shard_map/ppermute | solution.py:263
  26.4 7.3 %collective-permute-start.14 = (bf16[256,256]{1,0:T(8,128)(2,1)S(1)}, bf16[256,256]{1,0:T(8,128)(2,1)S(1)}, u32[]{:S(2)}, u32[]{:S(2)}) collective-permute-start(bf16[256,256]{1,0:T(8,128)(2,1)S(1)} %shard_map.91), channel_id=1, source_target_pairs={{0,15},{1,2},{2,1},{3,4},{4,3},{5,6},{6,5},{7,8},{8,7},{9,10},{10,... | collective-permute-start | bytes 393224 | tf_op jit(solution)/shard_map/ppermute | solution.py:267
  33.7 8.6 %collective-permute-start.18 = (bf16[256,256]{1,0:T(8,128)(2,1)S(1)}, bf16[256,256]{1,0:T(8,128)(2,1)S(1)}, u32[]{:S(2)}, u32[]{:S(2)}) collective-permute-start(bf16[256,256]{1,0:T(8,128)(2,1)S(1)} %get-tuple-element.62.refs_3_.refs_4_.refs_0_), channel_id=1, source_target_pairs={{0,8},{1,9},{2,10},{3,11},{4,12},{5,13},{6,14},{7,15},{8,0},{9,1},... | collective-permute-start | bytes 393224 | tf_op jit(solution)/shard_map/ppermute | solution.py:263
  36.5 7.2 %collective-permute-start.21 = (bf16[256,256]{1,0:T(8,128)(2,1)S(1)}, bf16[256,256]{1,0:T(8,128)(2,1)S(1)}, u32[]{:S(2)}, u32[]{:S(2)}) collective-permute-start(bf16[256,256]{1,0:T(8,128)(2,1)S(1)} %get-tuple-element.62.refs_3_.refs_4_.refs_0_), channel_id=1, source_target_pairs={{0,4},{1,5},{2,6},{3,7},{4,0},{5,1},{6,2},{7,3},{8,12},{9,13},{10,... | collective-permute-start | bytes 393224 | tf_op jit(solution)/shard_map/ppermute | solution.py:263
  37.6 8.1 %collective-permute-start.20 = (bf16[256,256]{1,0:T(8,128)(2,1)S(1)}, bf16[256,256]{1,0:T(8,128)(2,1)S(1)}, u32[]{:S(2)}, u32[]{:S(2)}) collective-permute-start(bf16[256,256]{1,0:T(8,128)(2,1)S(1)} %get-tuple-element.62.refs_3_.refs_4_.refs_0_), channel_id=1, source_target_pairs={{0,2},{1,3},{2,0},{3,1},{4,6},{5,7},{6,4},{7,5},{8,10},{9,11},{10,... | collective-permute-start | bytes 393224 | tf_op jit(solution)/shard_map/ppermute | solution.py:263
  37.6 8.6 %collective-permute-start.17 = (bf16[256,256]{1,0:T(8,128)(2,1)S(1)}, bf16[256,256]{1,0:T(8,128)(2,1)S(1)}, u32[]{:S(2)}, u32[]{:S(2)}) collective-permute-start(bf16[256,256]{1,0:T(8,128)(2,1)S(1)} %get-tuple-element.62.refs_3_.refs_4_.refs_0_), channel_id=1, source_target_pairs={{0,6},{1,7},{2,4},{3,5},{4,2},{5,3},{6,0},{7,1},{8,14},{9,15},{10,... | collective-permute-start | bytes 393224 | tf_op jit(solution)/shard_map/ppermute | solution.py:263
  40.0 6.2 %collective-permute-start.16 = (bf16[256,256]{1,0:T(8,128)(2,1)S(1)}, bf16[256,256]{1,0:T(8,128)(2,1)S(1)}, u32[]{:S(2)}, u32[]{:S(2)}) collective-permute-start(bf16[256,256]{1,0:T(8,128)(2,1)S(1)} %get-tuple-element.62.refs_3_.refs_4_.refs_0_), channel_id=1, source_target_pairs={{0,1},{1,0},{2,3},{3,2},{4,5},{5,4},{6,7},{7,6},{8,9},{9,8},{10,11... | collective-permute-start | bytes 393224 | tf_op jit(solution)/shard_map/ppermute | solution.py:263
  42.3 7.3 %collective-permute-start.27 = (bf16[256,256]{1,0:T(8,128)(2,1)S(1)}, bf16[256,256]{1,0:T(8,128)(2,1)S(1)}, u32[]{:S(2)}, u32[]{:S(2)}) collective-permute-start(bf16[256,256]{1,0:T(8,128)(2,1)S(1)} %shard_map.97.refs_0_.refs_10_.refs_11_.refs_7_), channel_id=1, source_target_pairs={{0,6},{1,7},{2,4},{3,5},{4,2},{5,3},{6,0},{7,1},{8,14},{9,15},{10,... | collective-permute-start | bytes 393224 | tf_op jit(solution)/shard_map/ppermute | solution.py:263
  43.7 7.9 %collective-permute-start.25 = (bf16[256,256]{1,0:T(8,128)(2,1)S(1)}, bf16[256,256]{1,0:T(8,128)(2,1)S(1)}, u32[]{:S(2)}, u32[]{:S(2)}) collective-permute-start(bf16[256,256]{1,0:T(8,128)(2,1)S(1)} %shard_map.97.refs_0_.refs_10_.refs_11_.refs_7_), channel_id=1, source_target_pairs={{0,4},{1,5},{2,6},{3,7},{4,0},{5,1},{6,2},{7,3},{8,12},{9,13},{10,... | collective-permute-start | bytes 393224 | tf_op jit(solution)/shard_map/ppermute | solution.py:263
  45.7 6.0 %collective-permute-start.23 = (bf16[256,256]{1,0:T(8,128)(2,1)S(1)}, bf16[256,256]{1,0:T(8,128)(2,1)S(1)}, u32[]{:S(2)}, u32[]{:S(2)}) collective-permute-start(bf16[256,256]{1,0:T(8,128)(2,1)S(1)} %shard_map.97.refs_0_.refs_10_.refs_11_.refs_7_), channel_id=1, source_target_pairs={{0,2},{1,3},{2,0},{3,1},{4,6},{5,7},{6,4},{7,5},{8,10},{9,11},{10,... | collective-permute-start | bytes 393224 | tf_op jit(solution)/shard_map/ppermute | solution.py:263
  46.2 6.9 %collective-permute-start.22 = (bf16[512,256]{1,0:T(8,128)(2,1)S(1)}, bf16[512,256]{1,0:T(8,128)(2,1)S(1)}, u32[]{:S(2)}, u32[]{:S(2)}) collective-permute-start(bf16[512,256]{1,0:T(8,128)(2,1)S(1)} %shard_map.99), channel_id=1, source_target_pairs={{0,1},{1,0},{2,3},{3,2},{4,5},{5,4},{6,7},{7,6},{8,9},{9,8},{10,11... | collective-permute-start | bytes 786440 | tf_op jit(solution)/shard_map/ppermute | solution.py:263
  46.2 6.9 %collective-permute-start.19 = (bf16[512,256]{1,0:T(8,128)(2,1)S(1)}, bf16[512,256]{1,0:T(8,128)(2,1)S(1)}, u32[]{:S(2)}, u32[]{:S(2)}) collective-permute-start(bf16[512,256]{1,0:T(8,128)(2,1)S(1)} %shard_map.98), channel_id=1, source_target_pairs={{0,1},{1,0},{2,3},{3,2},{4,5},{5,4},{6,7},{7,6},{8,9},{9,8},{10,11... | collective-permute-start | bytes 786440 | tf_op jit(solution)/shard_map/ppermute | solution.py:263
  54.2 9.6 %collective-permute-start.29 = (bf16[256,256]{1,0:T(8,128)(2,1)S(1)}, bf16[256,256]{1,0:T(8,128)(2,1)S(1)}, u32[]{:S(2)}, u32[]{:S(2)}) collective-permute-start(bf16[256,256]{1,0:T(8,128)(2,1)S(1)} %shard_map.100), channel_id=1, source_target_pairs={{0,8},{1,9},{2,10},{3,11},{4,12},{5,13},{6,14},{7,15},{8,0},{9,1},... | collective-permute-start | bytes 393224 | tf_op jit(solution)/shard_map/ppermute | solution.py:263
  56.3 7.5 %collective-permute-start.30 = (bf16[256,256]{1,0:T(8,128)(2,1)S(1)}, bf16[256,256]{1,0:T(8,128)(2,1)S(1)}, u32[]{:S(2)}, u32[]{:S(2)}) collective-permute-start(bf16[256,256]{1,0:T(8,128)(2,1)S(1)} %shard_map.101), channel_id=1, source_target_pairs={{0,15},{1,2},{2,1},{3,4},{4,3},{5,6},{6,5},{7,8},{8,7},{9,10},{10,... | collective-permute-start | bytes 393224 | tf_op jit(solution)/shard_map/ppermute | solution.py:267
  (9 other events, 19.1 us)
